TPU v7x, 128 devices: a whole 4x4x4 slice. The times are simulated.
128 devices in a mesh: dp: 4 (over y_hi, core), seq: 32 (over x, z, y_lo).
Axes of the slice: x: 4, y: 4 (y_hi: 2, y_lo: 2; y = y_hi * 2 + y_lo), z: 4, core: 2. Of those that a mesh axis runs over, the one named last changes fastest.
Arguments:
- images: bfloat16 [4, 3, 1024, 1024], P('dp', None, 'seq'), may hold values from -6 to 6
- boxes: int32 [4, 4], replicated, may hold values from 0 to 1024, as said below
- w_embed: bfloat16 [588, 1280], replicated, may hold values from -0.25 to 0.25
- pos_embed: bfloat16 [4096, 1280], P('seq'), may hold values from -3 to 3
- gain_attn: float32 [1280], replicated, may hold values from 0.1 to 1.9
- w_qkv: bfloat16 [1280, 3840], replicated, as said below
- w_attn_out: bfloat16 [1280, 1280], replicated, may hold values from -0.15625 to 0.15625
- gain_mlp: float32 [1280], replicated, may hold values from 0.1 to 1.9
- w_up: bfloat16 [1280, 5120], P(None, 'dp'), may hold values from -0.15625 to 0.15625
- w_down: bfloat16 [5120, 1280], P('dp'), may hold values from -0.078125 to 0.078125
Outputs:
- encoded: bfloat16 [4, 4096, 1280], P('dp', 'seq')
Inputs may be any that keep to these rules, and one draw needn't show every extreme that they name: `boxes`: each row is (top, left, height, width) of a crop inside the 1024 x 1024 source image, with height and width at least 512; in every draw some image's box is the whole source image and another image's box is the lower right quarter (top and left 1024 // 2, height and width 1024 // 2). `w_qkv`: columns are the query, key and value projections in that order.
All inputs are finite; a program needn't handle non-finite values.
Results may differ from a plain program's by a relative error of at most 0.04.
Values may be sent and summed in bfloat16 or wider, within the bound.
A program may use at most 192 MiB of HBM per device.

v0:
```python
import math

import jax
import jax.numpy as jnp
from jax import lax
from jax.sharding import PartitionSpec as P

HEADS = 16
PATCH = 14


def bilinear(first, length, targets, sources, extent):
    numer = (2 * targets + 1) * length - extent
    lower = jnp.where(numer < 0, 0, numer // (2 * extent))
    remain = jnp.where(numer < 0, 0, numer - lower * 2 * extent)
    fraction = remain.astype(jnp.float32) / (2.0 * extent)
    upper = jnp.minimum(lower + 1, length - 1)
    near_hit = (sources[None, :] == (first + lower)[:, None]).astype(jnp.float32)
    far_hit = (sources[None, :] == (first + upper)[:, None]).astype(jnp.float32)
    return (1.0 - fraction)[:, None] * near_hit + fraction[:, None] * far_hit


def layer_norm(values, gain):
    center = values - jnp.mean(values, axis=-1, keepdims=True)
    spread = jnp.mean(center * center, axis=-1, keepdims=True)
    return (center * lax.rsqrt(spread + 1e-06) * gain).astype(jnp.bfloat16)


def shards(images, boxes, w_embed, pos_embed, gain_attn, w_qkv, w_attn_out, gain_mlp, w_up, w_down):
    parts = lax.axis_size("seq")
    rank = lax.axis_index("seq")
    tokens_dev = pos_embed.shape[0]
    width = pos_embed.shape[1]
    side = math.isqrt(tokens_dev * parts)
    rows_dev = tokens_dev // side
    out_px = side * PATCH
    source_px = images.shape[3]
    crop_box = boxes[lax.axis_index("dp")]
    band = rows_dev * PATCH
    targets = rank * band + jnp.arange(band, dtype=jnp.int32)
    sources = jnp.arange(source_px, dtype=jnp.int32)
    row_weights = bilinear(crop_box[0], crop_box[2], targets, sources, out_px)
    col_weights = bilinear(
        crop_box[1], crop_box[3], jnp.arange(out_px, dtype=jnp.int32), sources, out_px
    )
    picture = images[0]
    channels = picture.shape[0]
    rowed = jnp.einsum(
        "or,crq->coq",
        row_weights,
        lax.all_gather(picture, "seq", axis=1, tiled=True).astype(jnp.float32),
        precision=lax.Precision.HIGH,
    )
    resampled = jnp.einsum("coq,pq->cop", rowed, col_weights, precision=lax.Precision.HIGH)
    patches = resampled.astype(jnp.bfloat16).reshape(channels, rows_dev, PATCH, side, PATCH)
    patches = patches.transpose(1, 3, 0, 2, 4).reshape(tokens_dev, channels * PATCH * PATCH)
    embedded = jnp.dot(patches, w_embed, preferred_element_type=jnp.float32) + pos_embed.astype(
        jnp.float32
    )
    normed_attn = layer_norm(embedded, gain_attn)
    projected = jnp.dot(normed_attn, w_qkv, preferred_element_type=jnp.float32).astype(jnp.bfloat16)
    queries = projected[:, :width]
    keyset = projected[:, width : 2 * width]
    valueset = projected[:, 2 * width :]
    head_size = width // HEADS
    inverse = 1.0 / math.sqrt(head_size)
    query_heads = queries.reshape(tokens_dev, HEADS, head_size)
    running_max = jnp.full((HEADS, tokens_dev), -jnp.inf, jnp.float32)
    running_sum = jnp.zeros((HEADS, tokens_dev), jnp.float32)
    running_acc = jnp.zeros((HEADS, tokens_dev, head_size), jnp.float32)
    key_piece = lax.all_gather(keyset, "seq", axis=0, tiled=True)
    value_piece = lax.all_gather(valueset, "seq", axis=0, tiled=True)
    count = key_piece.shape[0]
    key_heads = key_piece.reshape(count, HEADS, head_size)
    value_heads = value_piece.reshape(count, HEADS, head_size)
    scores = (
        jnp.einsum("qhd,khd->hqk", query_heads, key_heads, preferred_element_type=jnp.float32)
        * inverse
    )
    new_max = jnp.max(scores, axis=2)
    correction = jnp.exp(running_max - new_max)
    unnormed = jnp.exp(scores - new_max[:, :, None])
    new_sum = running_sum * correction + jnp.sum(unnormed, axis=2)
    product = jnp.einsum(
        "hqk,khd->hqd",
        unnormed.astype(jnp.bfloat16),
        value_heads,
        preferred_element_type=jnp.float32,
    )
    final_acc = running_acc * correction[:, :, None] + product
    attended = (final_acc / new_sum[:, :, None]).astype(jnp.bfloat16)
    attended = attended.transpose(1, 0, 2).reshape(tokens_dev, width)
    middle = embedded + jnp.dot(attended, w_attn_out, preferred_element_type=jnp.float32)
    normed_mlp = layer_norm(middle, gain_mlp)
    gathered = lax.all_gather(normed_mlp, "dp", axis=0, tiled=True)
    hidden = jax.nn.gelu(
        jnp.dot(gathered, w_up, preferred_element_type=jnp.float32), approximate=False
    ).astype(jnp.bfloat16)
    mixed = lax.psum_scatter(
        jnp.dot(hidden, w_down, preferred_element_type=jnp.float32).astype(jnp.bfloat16),
        "dp",
        scatter_dimension=0,
        tiled=True,
    ).astype(jnp.float32)
    return (middle + mixed).astype(jnp.bfloat16)[None]


def solution(mesh):
    return jax.shard_map(
        shards,
        mesh=mesh,
        in_specs=(
            P("dp", None, "seq", None),
            P(),
            P(),
            P("seq", None),
            P(),
            P(),
            P(),
            P(),
            P(None, "dp"),
            P("dp", None),
        ),
        out_specs=P("dp", "seq", None),
        check_vma=False,
    )
```

profile of v0, /device:TPU:0, one launch (start us, length us, event | category | flops | bytes accessed | tf_op | source)
XLA Modules:
  0.0 774.1 jit_solution(3165919515998093857)
XLA Ops:
  6.5 0.7 all-gather.12.cloned.1.call-update
  7.3 0.9 constant_dynamic-slice_fusion
  8.2 0.7 fusion.131
  10.1 0.7 broadcast_subtract_fusion.1
  10.8 1.3 minimum_add_fusion.1
  12.1 0.6 convert_multiply_fusion
  12.7 1.3 minimum_add_fusion
  14.0 162.1 %all-gather.12.cloned.1.call-done = bf16[1,3,1024,1024]{3,2,1,0:T(8,128)(2,1)} async-done(((bf16[1,3,32,1024]{3,2,1,0:T(8,128)(2,1)}), bf16[1,3,1024,1024]{3,2,1,0:T(8,128)(2,1)}) %all-gather.12.cloned.1.call-update) | async-done | bytes 6291472 | tf_op jit(solution)/shard_map/all_gather | solution.py:51
  176.1 5.0 fusion.62
  181.1 2.4 fusion.68
  183.5 4.3 reshape.130
  187.8 2.5 copy.14
  190.3 1.2 reshape.131
  191.5 2.0 fusion.132
  193.7 5.3 convolution_convert_fusion
  199.0 1.0 fusion.130
  200.1 0.7 all-gather.8.cloned.1.call-update
  201.0 1.9 copy.15
  202.9 228.9 %all-gather.6.cloned.1.call-done = bf16[4096,1280]{1,0:T(8,128)(2,1)} async-done(((bf16[128,1280]{1,0:T(8,128)(2,1)}), bf16[4096,1280]{1,0:T(8,128)(2,1)}) %all-gather.6.cloned.1.call-update) | async-done | bytes 10485776 | tf_op jit(solution)/shard_map/all_gather | solution.py:71
  431.8 14.3 %copy.16 = bf16[4096,1280]{0,1:T(8,128)(2,1)} copy(bf16[4096,1280]{1,0:T(8,128)(2,1)} %all-gather.6.cloned.1.call-done) | data formatting | bytes 20971520 | tf_op jit(solution)/shard_map/all_gather | solution.py:71
  446.1 16.0 %multiply_reduce_fusion = (f32[16,128]{1,0:T(8,128)S(1)}, f32[16,128,4096]{2,1,0:T(8,128)}) fusion(bf16[128,16,80]{0,2,1:T(8,128)(2,1)} %bitcast.57, bf16[4096,16,80]{0,2,1:T(8,128)(2,1)} %bitcast.54), kind=kOutput, calls=%fused_computation.1 | convolution fusion | flops 1358952448 | bytes 44376064 | tf_op jit(solution)/shard_map/qhd,khd->hqk/dot_general | solution.py:77
  462.1 14.1 %fusion = f32[16,128]{1,0:T(8,128)S(1)} fusion(f32[16,128,4096]{2,1,0:T(8,128)} %get-tuple-element.17, f32[16,128]{1,0:T(8,128)S(1)} %get-tuple-element.16), kind=kLoop, calls=%fused_computation.2 | loop fusion | flops 25163776 | bytes 33570816 | tf_op jit(solution)/shard_map/reduce_sum | solution.py:83
  476.2 188.8 %all-gather.8.cloned.1.call-done = bf16[4096,1280]{1,0:T(8,128)(2,1)} async-done(((bf16[128,1280]{1,0:T(8,128)(2,1)}), bf16[4096,1280]{1,0:T(8,128)(2,1)}) %all-gather.8.cloned.1.call-update) | async-done | bytes 10485776 | tf_op jit(solution)/shard_map/all_gather | solution.py:72
  665.0 14.3 %copy.17 = bf16[4096,1280]{0,1:T(8,128)(2,1)} copy(bf16[4096,1280]{1,0:T(8,128)(2,1)} %all-gather.8.cloned.1.call-done) | data formatting | bytes 20971520 | tf_op jit(solution)/shard_map/all_gather | solution.py:72
  679.3 16.4 %fusion.74 = bf16[128,16,80]{0,2,1:T(8,128)(2,1)S(1)} fusion(bf16[4096,16,80]{0,2,1:T(8,128)(2,1)} %bitcast.55, f32[16,128,4096]{2,1,0:T(8,128)} %get-tuple-element.17, f32[16,128]{1,0:T(8,128)S(1)} %get-tuple-element.16, f32[128,16]{0,1:T(8,128)S(1)} %bitcast_add_fusion, f32[128,16]{0,1:T(8,128)S(1)} %multiply_bitcast_fusion), kind=kOutput, calls=%fused_computation.79 | convolution fusion | flops 1367834624 | bytes 44392448 | tf_op jit(solution)/shard_map/hqk,khd->hqd/dot_general | solution.py:84
  695.8 0.7 fusion.133
  696.8 0.6 copy-done.3
  697.4 0.9 multiply_convert_fusion
  698.6 22.3 %all-gather.10.cloned.1.call-done = bf16[512,1280]{1,0:T(8,128)(2,1)} async-done(((bf16[128,1280]{1,0:T(8,128)(2,1)}), bf16[512,1280]{1,0:T(8,128)(2,1)}) %all-gather.10.cloned.1.call-update) | async-done | bytes 1310736 | tf_op jit(solution)/shard_map/all_gather | solution.py:95
  720.9 11.7 %convolution_convert_fusion.1 = bf16[512,1280]{1,0:T(8,128)(2,1)} fusion(bf16[1280,1280]{1,0:T(8,128)(2,1)S(1)} %copy-done, bf16[512,1280]{1,0:T(8,128)(2,1)} %all-gather.10.cloned.1.call-done, bf16[1280,1280]{1,0:T(8,128)(2,1)} %param.18), kind=kOutput, calls=%fused_computation.18 | convolution fusion | flops 3398696960 | bytes 9175040 | tf_op jit(solution)/shard_map/dot_general | solution.py:100
  732.6 33.0 %reduce-scatter.2.cloned.1.call-done = bf16[128,1280]{1,0:T(8,128)(2,1)} async-done(((bf16[512,1280]{1,0:T(8,128)(2,1)}), bf16[128,1280]{1,0:T(8,128)(2,1)}) %reduce-scatter.2.cloned.1.call-update) | async-done | bytes 327696 | tf_op jit(solution)/shard_map/reduce_scatter | solution.py:99
  765.6 1.9 fusion.77
  (29 shorter events, 1.1 us)
Async XLA Ops:
  6.5 714.3 %copy-start = (bf16[1280,1280]{1,0:T(8,128)(2,1)S(1)}, bf16[1280,1280]{1,0:T(8,128)(2,1)}, u32[]{:S(2)}) copy-start(bf16[1280,1280]{1,0:T(8,128)(2,1)} %param.19) | copy-start | bytes 9830404
  6.5 169.6 %all-gather.12.cloned.1.call-start = ((), (), s32[]{:S(2)}) async-start(), calls=%async_computation.5 | async-start | bytes 6488064 | tf_op jit(solution)/shard_map/all_gather | solution.py:51
  7.3 424.5 %all-gather.6.cloned.1.call-start = ((), (), s32[]{:S(2)}) async-start(), calls=%async_computation.1 | async-start | bytes 10813440 | tf_op jit(solution)/shard_map/all_gather | solution.py:71
  187.8 5.8 copy-start.5
  193.4 5.6 copy-start.1
  200.0 465.0 %all-gather.8.cloned.1.call-start = ((), (), s32[]{:S(2)}) async-start(), calls=%async_computation.2 | async-start | bytes 10813440 | tf_op jit(solution)/shard_map/all_gather | solution.py:72
  200.8 520.1 %all-gather.10.cloned.1.call-start = ((), (), s32[]{:S(2)}) async-start(), calls=%async_computation.3 | async-start | bytes 1638400 | tf_op jit(solution)/shard_map/all_gather | solution.py:95
  679.3 16.4 %copy-start.2 = (f32[128,1280]{1,0:T(8,128)S(1)}, f32[128,1280]{1,0:T(8,128)}, u32[]{:S(2)}) copy-start(f32[128,1280]{1,0:T(8,128)} %copy-done.1) | copy-start | bytes 1966084
  679.3 16.5 %copy-start.4 = (bf16[1280,1280]{1,0:T(8,128)(2,1)S(1)}, bf16[1280,1280]{1,0:T(8,128)(2,1)}, u32[]{:S(2)}) copy-start(bf16[1280,1280]{1,0:T(8,128)(2,1)} %param.16) | copy-start | bytes 9830404
  695.8 1.6 copy-start.6
  696.5 0.8 copy-start.3
  698.3 67.3 %reduce-scatter.2.cloned.1.call-start = ((), (), s32[]{:S(2)}) async-start(), calls=%async_computation.4 | async-start | bytes 1638400 | tf_op jit(solution)/shard_map/reduce_scatter | solution.py:99
Sparse Core Ops, SparseCore 0:
  9.0 167.0 all-gather.11
  200.1 231.5 all-gather.5
  433.4 231.5 all-gather.7
  698.4 22.3 all-gather.9
  732.7 32.8 reduce-scatter.1
where the time goes:
time: 776 us; the launch traced here: 774 us
  waiting for transfers between devices  637 us (82%)
  matrix products  59.6 us (8%)
  local copies, waits for them, and re-layouts  41.6 us (5%)
  other arithmetic  21.3 us (3%)
  between operations  14.5 us (2%)
    all_gather x1, waiting for transfers between devices, shards(): key_piece = lax.all_gather(keyset, 'seq', axis=0, tiled=True)  229 us
    all_gather x1, waiting for transfers between devices, shards(): value_piece = lax.all_gather(valueset, 'seq', axis=0, tiled=True)  189 us
    all_gather x1, waiting for transfers between devices, shards(): lax.all_gather(picture, 'seq', axis=1, tiled=True).astype(jnp.float32)  162 us
    reduce_scatter x1, waiting for transfers between devices, shards(): lax.psum_scatter(jnp.dot(hidden, w_down, preferred_element_type=jnp.float...  33 us
    all_gather x1, waiting for transfers between devices, shards(): gathered = lax.all_gather(normed_mlp, 'dp', axis=0, tiled=True)  22.3 us
    dot_general x1, matrix products, shards(): jnp.einsum('hqk,khd->hqd', unnormed.astype(jnp.bfloat16), value_heads, pr...  16.4 us
    dot_general x1, matrix products, shards(): jnp.einsum('qhd,khd->hqk', query_heads, key_heads, preferred_element_type...  16 us
  transfers between devices with their start and end apart: 5, of which 5 were waited for; matrix products, arithmetic and copies ran while one was open for 7% of the time, Pallas kernels for 0%

commit v1 on v0

v1 whole, which is shorter than its diff:
```python
import functools
import math

import jax
import jax.numpy as jnp
from jax import lax
from jax.experimental import pallas as pl
from jax.experimental.pallas import tpu as pltpu
from jax.sharding import PartitionSpec as P

HEADS = 16
HEAD = 80
PATCH = 14
OUT = 896
SEQ = 32
TOK = 128
WIDTH = 1280
MESH = pl.DeviceIdType.MESH
F32 = jnp.float32
BF16 = jnp.bfloat16


def taps(o, valid, first, length):
    numer = ((2 * o + 1) * length - OUT).astype(F32)
    lower = jnp.floor(numer * (1.0 / (2 * OUT)))
    remain = numer - lower * (2.0 * OUT)
    lower = jnp.where(remain < 0, lower - 1.0, jnp.where(remain >= 2.0 * OUT, lower + 1.0, lower))
    remain = numer - lower * (2.0 * OUT)
    lower = jnp.where(numer < 0, 0.0, lower).astype(jnp.int32)
    share = jnp.where(numer < 0, 0.0, remain) * (1.0 / (2 * OUT))
    upper = jnp.minimum(lower + 1, length - 1)
    near = jnp.where(valid, first + lower, -1)
    far = jnp.where(valid, first + upper, -1)
    return near, far, share


def resample_kernel(boxes, img, out, wcol, cmat, send1, recv1, wrow, send2, recv2, wide, s1, r1, s2, r2):
    dp, me = lax.axis_index("dp"), lax.axis_index("seq")
    barrier = pltpu.get_barrier_semaphore()

    @pl.loop(1, SEQ)
    def _(k):
        pl.semaphore_signal(barrier, inc=1, device_id=(dp, lax.rem(me + k, SEQ)), device_id_type=MESH)

    top, left, height, width = boxes[dp, 0], boxes[dp, 1], boxes[dp, 2], boxes[dp, 3]

    @pl.loop(0, 8)
    def _(t):
        lane = lax.broadcasted_iota(jnp.int32, (8, 128), 1)
        half, d4, j = lane // 64, (lane % 64) // 16, lane % 16
        o = (t * 4 + d4) * 28 + half * 14 + j
        near, far, share = taps(o, j < 14, left, width)
        near, far, share = near[:1], far[:1], share[:1]
        row = lax.broadcasted_iota(jnp.int32, (1024, 128), 0)
        w = jnp.where(row == near, 1.0 - share, 0.0) + jnp.where(row == far, share, 0.0)
        wcol[:, pl.ds(pl.multiple_of(t * 128, 128), 128)] = w.astype(BF16)

    cmat[...] = jnp.dot(img[...], wcol[...], preferred_element_type=F32)

    @pl.loop(0, 8)
    def _(t):
        cols = pl.ds(pl.multiple_of(t * 128, 128), 128)
        lane = lax.broadcasted_iota(jnp.int32, (32, 128), 1)
        group = (lane % 64) // 16
        parts = [cmat[32 * ch : 32 * ch + 32, cols] for ch in range(3)]
        for d4 in range(4):
            chunk = jnp.zeros((32, 128), F32)
            for ch in range(3):
                shift = (16 * (ch - d4)) % 128
                moved = parts[ch] if shift == 0 else pltpu.roll(parts[ch], shift, 1)
                chunk = jnp.where(group == ch, moved, chunk)
            send1[t * 4 + d4] = chunk.astype(BF16)

    def first(dst, src):
        return pltpu.make_async_remote_copy(
            src_ref=send1.at[dst], dst_ref=recv1.at[src], send_sem=s1.at[dst], recv_sem=r1.at[src],
            device_id=(dp, dst), device_id_type=MESH)

    def second(dst, src):
        return pltpu.make_async_remote_copy(
            src_ref=send2.at[dst], dst_ref=recv2.at[src], send_sem=s2.at[dst], recv_sem=r2.at[src],
            device_id=(dp, dst), device_id_type=MESH)

    pl.semaphore_wait(barrier, SEQ - 1)

    @pl.loop(1, SEQ)
    def _(k):
        first(lax.rem(me + k, SEQ), me).start()

    recv1[me] = send1[me]

    @pl.loop(0, 8)
    def _(t):
        row = lax.broadcasted_iota(jnp.int32, (128, 128), 0) + t * 128
        odd, d, kt, a2 = row // 512, (row % 512) // 16, (row % 16) // 2, row % 2
        o = (2 * d + a2) * 14 + 2 * kt + odd
        near, far, share = taps(o, kt < 7, top, height)
        rows = pl.ds(pl.multiple_of(t * 128, 128), 128)
        for c in range(8):
            col = lax.broadcasted_iota(jnp.int32, (128, 128), 1) + c * 128
            w = jnp.where(col == near, 1.0 - share, 0.0) + jnp.where(col == far, share, 0.0)
            wrow[rows, c * 128 : c * 128 + 128] = w.astype(BF16)

    @pl.loop(1, SEQ)
    def _(k):
        first(me, lax.rem(me + k, SEQ)).wait_recv()

    x = recv1[...].reshape(1024, 128)
    even = jnp.dot(wrow[:512], x, preferred_element_type=F32)
    odd = jnp.dot(wrow[512:], x, preferred_element_type=F32)
    low = lax.broadcasted_iota(jnp.int32, (512, 128), 1) < 64
    send2[:, 0] = jnp.where(low, even, pltpu.roll(odd, 64, 1)).astype(BF16).reshape(32, 16, 128)
    send2[:, 1] = jnp.where(low, pltpu.roll(even, 64, 1), odd).astype(BF16).reshape(32, 16, 128)

    @pl.loop(1, SEQ)
    def _(k):
        second(lax.rem(me + k, SEQ), me).start()

    recv2[me] = send2[me]

    @pl.loop(1, SEQ)
    def _(k):
        first(lax.rem(me + k, SEQ), me).wait_send()
        second(me, lax.rem(me + k, SEQ)).wait_recv()

    wide[...] = recv2[...].reshape(1024, 128).astype(F32)
    for kt in range(7):
        for a2 in range(2):
            piece = wide[pl.ds(kt * 2 + a2, 64, stride=16), :]
            out[a2 * 64 : a2 * 64 + 64, kt * 128 : kt * 128 + 128] = piece.astype(BF16)

    @pl.loop(1, SEQ)
    def _(k):
        second(lax.rem(me + k, SEQ), me).wait_send()


def resample(boxes, img):
    return pl.pallas_call(
        resample_kernel,
        out_shape=jax.ShapeDtypeStruct((TOK, OUT), BF16),
        in_specs=[pl.BlockSpec(memory_space=pltpu.SMEM), pl.BlockSpec(memory_space=pltpu.VMEM)],
        out_specs=pl.BlockSpec(memory_space=pltpu.VMEM),
        scratch_shapes=[
            pltpu.VMEM((1024, 1024), BF16),
            pltpu.VMEM((96, 1024), F32),
            pltpu.VMEM((SEQ, 32, 128), BF16),
            pltpu.VMEM((SEQ, 32, 128), BF16),
            pltpu.VMEM((1024, 1024), BF16),
            pltpu.VMEM((SEQ, 2, 16, 128), BF16),
            pltpu.VMEM((SEQ, 2, 16, 128), BF16),
            pltpu.VMEM((1024, 128), F32),
            pltpu.SemaphoreType.DMA((SEQ,)),
            pltpu.SemaphoreType.DMA((SEQ,)),
            pltpu.SemaphoreType.DMA((SEQ,)),
            pltpu.SemaphoreType.DMA((SEQ,)),
        ],
        compiler_params=pltpu.CompilerParams(
            collective_id=0, has_side_effects=True, vmem_limit_bytes=48 * 1024 * 1024),
        name="resample",
    )(boxes, img)


QB = 256


def attend_kernel(proj, out, flat, mine, theirs, acc, peak, back, s_in, r_in, s_swap, r_swap, s_back, r_back):
    dp, me = lax.axis_index("dp"), lax.axis_index("seq")
    core, base = lax.rem(dp, 2), dp - lax.rem(dp, 2)
    half, slot = lax.rem(me, 2), me // 2
    image, head = me // 16, lax.rem(me, 16)
    to_dp, to_seq = base + half, core * 16
    from_dp = base + image
    sibling = base + 1 - core

    barrier = pltpu.get_barrier_semaphore()

    def is_me(d, s):
        return jnp.logical_and(d == dp, s == me)

    for h in range(HEADS):
        @pl.when(jnp.logical_not(is_me(to_dp, to_seq + h)))
        def _():
            pl.semaphore_signal(barrier, inc=1, device_id=(to_dp, to_seq + h), device_id_type=MESH)

        @pl.when(jnp.logical_not(is_me(from_dp, 2 * h + core)))
        def _():
            pl.semaphore_signal(barrier, inc=1, device_id=(from_dp, 2 * h + core), device_id_type=MESH)
    pl.semaphore_signal(barrier, inc=1, device_id=(sibling, me), device_id_type=MESH)

    mine[2, HEAD:, :] = jnp.ones((16, 2048), BF16)
    mine[1, HEAD:, :] = jnp.zeros((16, 2048), BF16)
    mine[0, HEAD:, :] = jnp.zeros((16, 2048), BF16)

    for t in range(3):
        for j in range(10):
            block = proj[:, t * WIDTH + j * 128 : t * WIDTH + j * 128 + 128].astype(F32)
            if t == 0:
                block = block * (math.log2(math.e) / math.sqrt(HEAD))
            flat[t, j * 128 : j * 128 + 128, :] = block.T.astype(BF16)

    self_head = jnp.logical_and(to_dp == dp, core == image)
    both = jnp.where(self_head, 2 * 15 + 1, 2 * 16 + 1)
    pl.semaphore_wait(barrier, both)

    def rows(h):
        return pl.ds(pl.multiple_of(h * HEAD, 16), HEAD)

    def lanes(i):
        return pl.ds(pl.multiple_of(i * TOK, TOK), TOK)

    def inward(h, i):
        return pltpu.make_async_remote_copy(
            src_ref=flat.at[:, rows(h), :], dst_ref=mine.at[:, pl.ds(0, HEAD), lanes(i)],
            send_sem=s_in.at[h], recv_sem=r_in.at[i],
            device_id=(to_dp, to_seq + h), device_id_type=MESH)

    def backward(i, h):
        return pltpu.make_async_remote_copy(
            src_ref=back.at[i], dst_ref=out.at[rows(h), :],
            send_sem=s_back.at[i], recv_sem=r_back.at[h],
            device_id=(from_dp, 2 * i + core), device_id_type=MESH)

    swap = pltpu.make_async_remote_copy(
        src_ref=mine.at[pl.ds(1, 2)], dst_ref=theirs, send_sem=s_swap, recv_sem=r_swap,
        device_id=(sibling, me), device_id_type=MESH)

    @pl.loop(0, HEADS)
    def _(k):
        h = lax.rem(slot + k, HEADS)

        @pl.when(is_me(to_dp, to_seq + h))
        def _():
            pltpu.make_async_copy(
                flat.at[:, rows(h), :], mine.at[:, pl.ds(0, HEAD), lanes(slot)], r_in.at[slot]).start()

        @pl.when(jnp.logical_not(is_me(to_dp, to_seq + h)))
        def _():
            inward(h, slot).start()

    @pl.loop(0, HEADS)
    def _(i):
        inward(0, i).wait_recv()

    swap.start()

    def scan(queries, keys, values):
        s = jnp.dot(queries, keys, preferred_element_type=F32)
        m = jnp.max(s, axis=1, keepdims=True)
        p = jnp.exp2(s - m).astype(BF16)
        o = lax.dot_general(p, values, (((1,), (1,)), ((), ())), preferred_element_type=F32)
        return m, o

    @pl.loop(0, 2048 // QB)
    def _(b):
        q = mine[0, :, pl.ds(pl.multiple_of(b * QB, QB), QB)].astype(F32).T.astype(BF16)
        m, o = scan(q, mine[1], mine[2])
        here = pl.ds(pl.multiple_of(b * QB, QB), QB)
        peak[here, :] = jnp.broadcast_to(m, (QB, 128))
        acc[here, :] = o

    swap.wait_recv()

    @pl.loop(0, 2048 // QB)
    def _(b):
        q = mine[0, :, pl.ds(pl.multiple_of(b * QB, QB), QB)].astype(F32).T.astype(BF16)
        m2, o2 = scan(q, theirs[0], theirs[1])
        here = pl.ds(pl.multiple_of(b * QB, QB), QB)
        m1 = peak[here, :][:, :1]
        o1 = acc[here, :]
        m = jnp.maximum(m1, m2)
        o = o1 * jnp.exp2(m1 - m) + o2 * jnp.exp2(m2 - m)
        o = o / o[:, HEAD : HEAD + 1]
        for j in range(QB // TOK):
            i = b * (QB // TOK) + j
            back[i] = o[j * TOK : j * TOK + TOK, :].T[:HEAD].astype(BF16)

            @pl.when(is_me(from_dp, 2 * i + core))
            def _():
                pltpu.make_async_copy(back.at[i], out.at[rows(head), :], r_back.at[head]).start()

            @pl.when(jnp.logical_not(is_me(from_dp, 2 * i + core)))
            def _():
                backward(i, head).start()

    swap.wait_send()

    @pl.loop(0, HEADS)
    def _(h):
        backward(0, h).wait_recv()

        @pl.when(jnp.logical_not(is_me(to_dp, to_seq + h)))
        def _():
            inward(h, 0).wait_send()

        @pl.when(jnp.logical_not(is_me(from_dp, 2 * h + core)))
        def _():
            backward(h, 0).wait_send()


def attend(proj):
    return pl.pallas_call(
        attend_kernel,
        out_shape=jax.ShapeDtypeStruct((WIDTH, TOK), BF16),
        in_specs=[pl.BlockSpec(memory_space=pltpu.VMEM)],
        out_specs=pl.BlockSpec(memory_space=pltpu.VMEM),
        scratch_shapes=[
            pltpu.VMEM((3, WIDTH, TOK), BF16),
            pltpu.VMEM((3, 96, 2048), BF16),
            pltpu.VMEM((2, 96, 2048), BF16),
            pltpu.VMEM((2048, 96), F32),
            pltpu.VMEM((2048, 128), F32),
            pltpu.VMEM((16, HEAD, TOK), BF16),
            pltpu.SemaphoreType.DMA((16,)),
            pltpu.SemaphoreType.DMA((16,)),
            pltpu.SemaphoreType.DMA,
            pltpu.SemaphoreType.DMA,
            pltpu.SemaphoreType.DMA((16,)),
            pltpu.SemaphoreType.DMA((16,)),
        ],
        compiler_params=pltpu.CompilerParams(
            collective_id=1, has_side_effects=True, vmem_limit_bytes=56 * 1024 * 1024),
        name="attend",
    )(proj)


def layer_norm(values, gain):
    center = values - jnp.mean(values, axis=-1, keepdims=True)
    spread = jnp.mean(center * center, axis=-1, keepdims=True)
    return (center * lax.rsqrt(spread + 1e-06) * gain).astype(BF16)


def shards(images, boxes, w_embed, pos_embed, gain_attn, w_qkv, w_attn_out, gain_mlp, w_up, w_down):
    tokens = resample(boxes, images.reshape(96, 1024))
    w = w_embed.reshape(3, PATCH, PATCH, WIDTH).transpose(1, 0, 2, 3)
    w = jnp.pad(w, ((0, 0), (0, 1), (0, 2), (0, 0))).reshape(OUT, WIDTH)
    embedded = jnp.dot(tokens, w, preferred_element_type=F32) + pos_embed.astype(F32)
    normed_attn = layer_norm(embedded, gain_attn)
    projected = jnp.dot(normed_attn, w_qkv, preferred_element_type=F32).astype(BF16)
    attended = attend(projected)
    middle = embedded + lax.dot_general(
        attended, w_attn_out, (((0,), (0,)), ((), ())), preferred_element_type=F32)
    normed_mlp = layer_norm(middle, gain_mlp)
    gathered = lax.all_gather(normed_mlp, "dp", axis=0, tiled=True)
    hidden = jax.nn.gelu(
        jnp.dot(gathered, w_up, preferred_element_type=F32), approximate=False).astype(BF16)
    mixed = lax.psum_scatter(
        jnp.dot(hidden, w_down, preferred_element_type=F32).astype(BF16),
        "dp", scatter_dimension=0, tiled=True).astype(F32)
    return (middle + mixed).astype(BF16)[None]


def solution(mesh):
    return jax.shard_map(
        shards,
        mesh=mesh,
        in_specs=(
            P("dp", None, "seq", None), P(), P(), P("seq", None), P(), P(), P(), P(),
            P(None, "dp"), P("dp", None),
        ),
        out_specs=P("dp", "seq", None),
        check_vma=False,
    )
```

time: 776 us -> 172 us (0.22)
  waiting for transfers between devices: 637 us -> 58 us
  Pallas kernels: 0 us -> 68.9 us
  matrix products: 59.6 us -> 20.4 us
  local copies, waits for them, and re-layouts: 41.6 us -> 6.62 us
  other arithmetic: 21.3 us -> 3.29 us
    all_gather x3 -> x0, waiting for transfers between devices: 580 us -> none  [the longest x1 229 us: shards(): key_piece = lax.all_gather(keyset, 'seq', axis=0, tiled=True)]
    pallas_call x0 -> x2, Pallas kernels: none -> 68.9 us  [the longest x1 45.7 us: attend(): pl.pallas_call(attend_kernel, out_shape=jax.ShapeDtypeStruct((WIDTH, TOK)...]
    dot_general x8 -> x4, matrix products: 59.6 us -> 20.4 us  [the longest x1 11.7 us: shards(): jnp.dot(hidden, w_down, preferred_element_type=F32).astype(BF16)]
    all_gather x2 -> x0, local copies, waits for them, and re-layouts: 28.6 us -> none  [the longest x1 14.3 us: shards(): key_piece = lax.all_gather(keyset, 'seq', axis=0, tiled=True)]
    reduce_sum x1 -> x0, other arithmetic: 14.1 us -> none  [shards(): new_sum = running_sum * correction + jnp.sum(unnormed, axis=2)]
  transfers between devices with their start and end apart: 5 -> 2, of which waited for: 5 -> 2; matrix products, arithmetic and copies ran while one was open for 7% -> 0% of each run, Pallas kernels for 0% -> 0%
where the time goes in v1:
time: 172 us; the launch traced here: 171 us
  Pallas kernels  68.9 us (40%)
  waiting for transfers between devices  58 us (34%)
  matrix products  20.4 us (12%)
  between operations  13.5 us (8%)
  local copies, waits for them, and re-layouts  6.62 us (4%)
  other arithmetic  3.29 us (2%)
    pallas_call x1, Pallas kernels, attend(): pl.pallas_call(attend_kernel, out_shape=jax.ShapeDtypeStruct((WIDTH, TOK)...  45.7 us
    reduce_scatter x1, waiting for transfers between devices, shards(): lax.psum_scatter(jnp.dot(hidden, w_down, preferred_element_type=F32).asty...  33 us
    all_gather x1, waiting for transfers between devices, shards(): gathered = lax.all_gather(normed_mlp, 'dp', axis=0, tiled=True)  24.9 us
    pallas_call x1, Pallas kernels, resample(): pl.pallas_call(resample_kernel, out_shape=jax.ShapeDtypeStruct((TOK, OUT)...  23.3 us
    dot_general x1, matrix products, shards(): jnp.dot(hidden, w_down, preferred_element_type=F32).astype(BF16)  11.7 us
    dot_general x1, matrix products, shards(): jnp.dot(normed_attn, w_qkv, preferred_element_type=F32).astype(BF16)  6.43 us
    reshape x1, local copies, waits for them, and re-layouts, shards(): w = w_embed.reshape(3, PATCH, PATCH, WIDTH).transpose(1, 0, 2, 3)  3.53 us
  transfers between devices with their start and end apart: 2, of which 2 were waited for; matrix products, arithmetic and copies ran while one was open for 0% of the time, Pallas kernels for 0%

profile of v1, /device:TPU:0, one launch (start us, length us, event | category | flops | bytes accessed | tf_op | source)
XLA Modules:
  0.0 171.0 jit_solution(14289103760398063919)
XLA Ops:
  6.5 0.0 copy-start
  6.5 0.0 all-gather.2.cloned.1.call-start
  6.5 3.5 %reshape.36 = bf16[3,14,14,1280]{3,2,1,0:T(8,128)(2,1)} reshape(bf16[588,1280]{1,0:T(8,128)(2,1)} %param.12) | data formatting | bytes 3010560 | tf_op jit(solution)/shard_map/reshape | solution.py:334
  10.1 1.6 copy.12
  11.6 0.0 copy-start.1
  11.7 0.0 copy-start.2
  11.7 0.0 copy-start.5
  11.7 0.3 pad.4.clone
  12.0 0.0 copy-start.6
  12.0 0.6 copy-done.1
  12.6 0.0 copy-done.2
  12.6 23.3 %resample.1 = bf16[128,896]{1,0:T(8,128)(2,1)S(1)} custom-call(s32[4,4]{1,0:T(4,128)S(1)} %copy-done.2, bf16[96,1024]{1,0:T(8,128)(2,1)S(1)} %bitcast.13), custom_call_target="tpu_custom_call" | custom-call | tf_op jit(solution)/shard_map/resample/pallas_call | solution.py:138
  35.9 0.0 copy-done.5
  35.9 0.6 fusion.75
  36.5 0.2 multiply_reduce_fusion.1
  36.7 0.0 copy-done.6
  36.7 0.0 copy-start.4
  36.7 6.4 %convolution_convert_fusion.proj = bf16[128,3840]{1,0:T(8,128)(2,1)} fusion(bf16[1280,3840]{1,0:T(8,128)(2,1)} %param.15, f32[128,1280]{1,0:T(8,128)S(1)} %get-tuple-element.6, f32[1280]{0:T(1024)S(1)} %copy-done.6, f32[128]{0:T(128)S(1)} %add_rsqrt_fusion.1, f32[128]{0:T(128)S(1)} %broadcast_multiply_fusion.1), kind=kOutput, calls=%fused_computation | convolution fusion | flops 1259438080 | bytes 11474944 | tf_op jit(solution)/shard_map/dot_general | solution.py:338
  43.2 45.7 %attend.1 = bf16[1280,128]{1,0:T(8,128)(2,1)} custom-call(bf16[128,3840]{1,0:T(8,128)(2,1)} %convolution_convert_fusion.proj), custom_call_target="tpu_custom_call" | custom-call | tf_op jit(solution)/shard_map/attend/pallas_call | solution.py:301
  88.8 0.0 copy-start.7
  88.9 1.7 fusion.76
  90.5 0.0 copy-start.3
  90.6 0.2 multiply_reduce_fusion
  90.8 0.6 copy-done.3
  91.4 0.9 multiply_convert_fusion
  92.3 0.0 all-gather.2.cloned.1.call-update
  92.3 0.2 reduce-scatter.2.cloned.1.call-start
  92.5 24.9 %all-gather.2.cloned.1.call-done = bf16[512,1280]{1,0:T(8,128)(2,1)} async-done(((bf16[128,1280]{1,0:T(8,128)(2,1)}), bf16[512,1280]{1,0:T(8,128)(2,1)}) %all-gather.2.cloned.1.call-update) | async-done | bytes 1310736 | tf_op jit(solution)/shard_map/all_gather | solution.py:343
  117.4 11.7 %convolution_convert_fusion.1 = bf16[512,1280]{1,0:T(8,128)(2,1)} fusion(bf16[1280,1280]{1,0:T(8,128)(2,1)S(1)} %copy-done, bf16[512,1280]{1,0:T(8,128)(2,1)} %all-gather.2.cloned.1.call-done, bf16[1280,1280]{1,0:T(8,128)(2,1)} %param.18), kind=kOutput, calls=%fused_computation.2 | convolution fusion | flops 3398696960 | bytes 9175040 | tf_op jit(solution)/shard_map/dot_general | solution.py:347
  129.2 0.0 reduce-scatter.2.cloned.1.call-update
  129.2 33.0 %reduce-scatter.2.cloned.1.call-done = bf16[128,1280]{1,0:T(8,128)(2,1)} async-done(((bf16[512,1280]{1,0:T(8,128)(2,1)}), bf16[128,1280]{1,0:T(8,128)(2,1)}) %reduce-scatter.2.cloned.1.call-update) | async-done | bytes 327696 | tf_op jit(solution)/shard_map/reduce_scatter | solution.py:346
  162.2 1.9 %fusion.41 = bf16[1,128,1280]{2,1,0:T(8,128)(2,1)} fusion(f32[128,1280]{1,0:T(8,128)} %copy-done.3, bf16[128,1280]{1,0:T(8,128)(2,1)} %reduce-scatter.2.cloned.1.call-done), kind=kLoop, calls=%fused_computation.58 | loop fusion | flops 491520 | bytes 1310720 | tf_op jit(solution)/shard_map/broadcast_in_dim | solution.py:349
  (7 shorter events, 0.0 us)
Async XLA Ops:
  6.5 110.9 %copy-start = (bf16[1280,1280]{1,0:T(8,128)(2,1)S(1)}, bf16[1280,1280]{1,0:T(8,128)(2,1)}, u32[]{:S(2)}) copy-start(bf16[1280,1280]{1,0:T(8,128)(2,1)} %param.19) | copy-start | bytes 9830404
  6.5 110.9 %all-gather.2.cloned.1.call-start = ((), (), s32[]{:S(2)}) async-start(), calls=%async_computation.1 | async-start | bytes 1638400 | tf_op jit(solution)/shard_map/all_gather | solution.py:343
  11.6 0.9 copy-start.1
  11.7 0.9 copy-start.2
  11.7 24.2 %copy-start.5 = (bf16[128,1280]{1,0:T(8,128)(2,1)S(1)}, bf16[128,1280]{1,0:T(8,128)(2,1)}, u32[]{:S(2)}) copy-start(bf16[128,1280]{1,0:T(8,128)(2,1)} %param.13) | copy-start | bytes 983044
  12.0 24.7 %copy-start.6 = (f32[1280]{0:T(1024)S(1)}, f32[1280]{0:T(1024)}, u32[]{:S(2)}) copy-start(f32[1280]{0:T(1024)} %param.14) | copy-start | bytes 15364
  36.7 52.1 %copy-start.4 = (bf16[1280,1280]{1,0:T(8,128)(2,1)S(1)}, bf16[1280,1280]{1,0:T(8,128)(2,1)}, u32[]{:S(2)}) copy-start(bf16[1280,1280]{1,0:T(8,128)(2,1)} %param.16) | copy-start | bytes 9830404
  88.8 2.6 %copy-start.7 = (f32[1280]{0:T(1024)S(1)}, f32[1280]{0:T(1024)}, u32[]{:S(2)}) copy-start(f32[1280]{0:T(1024)} %param.17) | copy-start | bytes 15364
  90.5 0.8 copy-start.3
  92.3 69.9 %reduce-scatter.2.cloned.1.call-start = ((), (), s32[]{:S(2)}) async-start(), calls=%async_computation.2 | async-start | bytes 1638400 | tf_op jit(solution)/shard_map/reduce_scatter | solution.py:346
Sparse Core Ops, SparseCore 0:
  92.4 24.9 all-gather.1
  129.3 32.8 reduce-scatter.1

commit v2 on v1

v2 whole, which is shorter than its diff:
```python
import math

import jax
import jax.numpy as jnp
from jax import lax
from jax.experimental import pallas as pl
from jax.experimental.pallas import tpu as pltpu
from jax.sharding import PartitionSpec as P

HEADS = 16
HEAD = 80
PATCH = 14
OUT = 896
SEQ = 32
TOK = 128
WIDTH = 1280
MESH = pl.DeviceIdType.MESH
F32 = jnp.float32
BF16 = jnp.bfloat16


def taps(o, valid, first, length):
    numer = ((2 * o + 1) * length - OUT).astype(F32)
    lower = jnp.floor(numer * (1.0 / (2 * OUT)))
    remain = numer - lower * (2.0 * OUT)
    lower = jnp.where(remain < 0, lower - 1.0, jnp.where(remain >= 2.0 * OUT, lower + 1.0, lower))
    remain = numer - lower * (2.0 * OUT)
    lower = jnp.where(numer < 0, 0.0, lower).astype(jnp.int32)
    share = jnp.where(numer < 0, 0.0, remain) * (1.0 / (2 * OUT))
    upper = jnp.minimum(lower + 1, length - 1)
    near = jnp.where(valid, first + lower, -1)
    far = jnp.where(valid, first + upper, -1)
    return near, far, share


def layer_norm(values, gain):
    center = values - jnp.mean(values, axis=-1, keepdims=True)
    spread = jnp.mean(center * center, axis=-1, keepdims=True)
    return (center * lax.rsqrt(spread + 1e-06) * gain).astype(BF16)


def gelu(x):
    return 0.5 * x * (1.0 + lax.erf(x * (1.0 / math.sqrt(2.0))))


QB = 256
CHUNKS = 2
ROWS = TOK // CHUNKS


def layer_kernel(
    boxes, images, w_embed, pos_embed, gain_attn, w_qkv, w_out, gain_mlp, w_up, w_down, result,
    img, emb, pos, qkv, outw, upw, downw, load,
    wcol, cmat, send1, recv1, wrow, send2, recv2, wide, tokens, embw, embedded, s1, r1, s2, r2,
    flat, mine, theirs, acc, peak, back, heads, s_in, r_in, s_swap, r_swap, s_back, r_back,
    normed, near_tok, far_tok, far_near, total, give, fromnear, giveswap, fromswap, giveback, fromfar,
    s_near, r_near, s_far, r_far, s_relay, r_relay, s_give, r_give, s_gs, r_gs, s_gb, r_gb,
):
    dp, me = lax.axis_index("dp"), lax.axis_index("seq")
    core, base = lax.rem(dp, 2), dp - lax.rem(dp, 2)
    half, slot = lax.rem(me, 2), me // 2
    image, head = me // 16, lax.rem(me, 16)
    to_dp, to_seq = base + half, core * 16
    from_dp = base + image
    sibling = (base + 1 - core, me)
    partner = (2 - base + core, me + 1 - 2 * half)

    def is_me(d, s):
        return jnp.logical_and(d == dp, s == me)

    loads = [
        pltpu.make_async_copy(a, b, load.at[i])
        for i, (a, b) in enumerate((
            (images.at[0, 0], img.at[pl.ds(0, 32)]), (images.at[0, 1], img.at[pl.ds(32, 32)]),
            (images.at[0, 2], img.at[pl.ds(64, 32)]), (w_embed, emb), (pos_embed, pos), (w_qkv, qkv),
            (w_out, outw), (w_up, upw), (w_down, downw)))
    ]
    for one in loads:
        one.start()

    barrier = pltpu.get_barrier_semaphore()

    def greet(d, s):
        pl.semaphore_signal(barrier, inc=1, device_id=(d, s), device_id_type=MESH)

    @pl.loop(1, SEQ)
    def _(k):
        greet(dp, lax.rem(me + k, SEQ))

    @pl.loop(0, HEADS)
    def _(h):
        @pl.when(jnp.logical_not(is_me(to_dp, to_seq + h)))
        def _():
            greet(to_dp, to_seq + h)

        @pl.when(jnp.logical_not(is_me(from_dp, 2 * h + core)))
        def _():
            greet(from_dp, 2 * h + core)

    greet(*sibling)
    greet(*partner)

    top, left, height, width = boxes[dp, 0], boxes[dp, 1], boxes[dp, 2], boxes[dp, 3]

    @pl.loop(0, 8)
    def _(t):
        lane = lax.broadcasted_iota(jnp.int32, (8, 128), 1)
        part, d4, j = lane // 64, (lane % 64) // 16, lane % 16
        o = (t * 4 + d4) * 28 + part * 14 + j
        near, far, share = taps(o, j < 14, left, width)
        near, far, share = near[:1], far[:1], share[:1]
        row = lax.broadcasted_iota(jnp.int32, (1024, 128), 0)
        w = jnp.where(row == near, 1.0 - share, 0.0) + jnp.where(row == far, share, 0.0)
        wcol[:, pl.ds(pl.multiple_of(t * 128, 128), 128)] = w.astype(BF16)

    for one in loads[:3]:
        one.wait()
    cmat[...] = jnp.dot(img[...], wcol[...], preferred_element_type=F32)

    @pl.loop(0, 8)
    def _(t):
        cols = pl.ds(pl.multiple_of(t * 128, 128), 128)
        lane = lax.broadcasted_iota(jnp.int32, (32, 128), 1)
        group = (lane % 64) // 16
        parts = [cmat[32 * ch : 32 * ch + 32, cols] for ch in range(3)]
        for d4 in range(4):
            chunk = jnp.zeros((32, 128), F32)
            for ch in range(3):
                shift = (16 * (ch - d4)) % 128
                moved = parts[ch] if shift == 0 else pltpu.roll(parts[ch], shift, 1)
                chunk = jnp.where(group == ch, moved, chunk)
            send1[t * 4 + d4] = chunk.astype(BF16)

    def first(dst, src):
        return pltpu.make_async_remote_copy(
            src_ref=send1.at[dst], dst_ref=recv1.at[src], send_sem=s1.at[dst], recv_sem=r1.at[src],
            device_id=(dp, dst), device_id_type=MESH)

    def second(dst, src):
        return pltpu.make_async_remote_copy(
            src_ref=send2.at[dst], dst_ref=recv2.at[src], send_sem=s2.at[dst], recv_sem=r2.at[src],
            device_id=(dp, dst), device_id_type=MESH)

    self_head = jnp.logical_and(half == core, core == image)
    pl.semaphore_wait(barrier, SEQ - 1 + 2 + jnp.where(self_head, 2 * 15, 2 * 16))

    @pl.loop(1, SEQ)
    def _(k):
        first(lax.rem(me + k, SEQ), me).start()

    recv1[me] = send1[me]

    @pl.loop(0, 8)
    def _(t):
        row = lax.broadcasted_iota(jnp.int32, (128, 128), 0) + t * 128
        odd, d, kt, a2 = row // 512, (row % 512) // 16, (row % 16) // 2, row % 2
        o = (2 * d + a2) * 14 + 2 * kt + odd
        near, far, share = taps(o, kt < 7, top, height)
        rows = pl.ds(pl.multiple_of(t * 128, 128), 128)
        for c in range(8):
            col = lax.broadcasted_iota(jnp.int32, (128, 128), 1) + c * 128
            w = jnp.where(col == near, 1.0 - share, 0.0) + jnp.where(col == far, share, 0.0)
            wrow[rows, c * 128 : c * 128 + 128] = w.astype(BF16)

    @pl.loop(1, SEQ)
    def _(k):
        first(me, lax.rem(me + k, SEQ)).wait_recv()

    x = recv1[...].reshape(1024, 128)
    even = jnp.dot(wrow[:512], x, preferred_element_type=F32)
    odd = jnp.dot(wrow[512:], x, preferred_element_type=F32)
    low = lax.broadcasted_iota(jnp.int32, (512, 128), 1) < 64
    send2[:, 0] = jnp.where(low, even, pltpu.roll(odd, 64, 1)).astype(BF16).reshape(32, 16, 128)
    send2[:, 1] = jnp.where(low, pltpu.roll(even, 64, 1), odd).astype(BF16).reshape(32, 16, 128)

    @pl.loop(1, SEQ)
    def _(k):
        second(lax.rem(me + k, SEQ), me).start()

    recv2[me] = send2[me]

    for one in loads[3:5]:
        one.wait()

    @pl.loop(0, 7)
    def _(t):
        rho = lax.broadcasted_iota(jnp.int32, (128, 588), 0) + t * 128
        i, ch, j = rho // 64, (rho % 64) // 16, rho % 16
        origin = jnp.where(jnp.logical_and(ch < 3, j < 14), ch * 196 + i * 14 + j, -1)
        kappa = lax.broadcasted_iota(jnp.int32, (128, 588), 1)
        pick = jnp.where(origin == kappa, 1.0, 0.0).astype(BF16)
        rows = pl.ds(pl.multiple_of(t * 128, 128), 128)
        embw[rows, :] = jnp.dot(pick, emb[...], preferred_element_type=F32).astype(BF16)

    mine[0, HEAD:, :] = jnp.zeros((16, 2048), BF16)
    mine[1, HEAD:, :] = jnp.zeros((16, 2048), BF16)
    mine[2, HEAD:, :] = jnp.ones((16, 2048), BF16)

    @pl.loop(1, SEQ)
    def _(k):
        first(lax.rem(me + k, SEQ), me).wait_send()
        second(me, lax.rem(me + k, SEQ)).wait_recv()

    wide[...] = recv2[...].reshape(1024, 128).astype(F32)
    for kt in range(7):
        for a2 in range(2):
            piece = wide[pl.ds(kt * 2 + a2, 64, stride=16), :]
            tokens[a2 * 64 : a2 * 64 + 64, kt * 128 : kt * 128 + 128] = piece.astype(BF16)

    embedded[...] = jnp.dot(tokens[...], embw[...], preferred_element_type=F32) + pos[...].astype(F32)
    normed[...] = layer_norm(embedded[...], gain_attn[...])

    def head_rows(h):
        return pl.ds(pl.multiple_of(h * HEAD, 16), HEAD)

    def lanes(i):
        return pl.ds(pl.multiple_of(i * TOK, TOK), TOK)

    def inward(t, h, i):
        return pltpu.make_async_remote_copy(
            src_ref=flat.at[t, head_rows(h), :], dst_ref=mine.at[t, pl.ds(0, HEAD), lanes(i)],
            send_sem=s_in.at[t, h], recv_sem=r_in.at[t, i],
            device_id=(to_dp, to_seq + h), device_id_type=MESH)

    def backward(i, h):
        return pltpu.make_async_remote_copy(
            src_ref=back.at[i], dst_ref=heads.at[head_rows(h), :],
            send_sem=s_back.at[i], recv_sem=r_back.at[h],
            device_id=(from_dp, 2 * i + core), device_id_type=MESH)

    loads[5].wait()
    for t in (1, 0, 2):
        proj = jnp.dot(normed[...], qkv[:, t * WIDTH : (t + 1) * WIDTH], preferred_element_type=F32)
        if t == 0:
            proj = proj * (math.log2(math.e) / math.sqrt(HEAD))
        for j in range(10):
            flat[t, j * 128 : j * 128 + 128, :] = proj[:, j * 128 : j * 128 + 128].T.astype(BF16)

        @pl.loop(0, HEADS)
        def _(k):
            h = lax.rem(slot + k, HEADS)

            @pl.when(is_me(to_dp, to_seq + h))
            def _():
                pltpu.make_async_copy(
                    flat.at[t, head_rows(h), :], mine.at[t, pl.ds(0, HEAD), lanes(slot)],
                    r_in.at[t, slot]).start()

            @pl.when(jnp.logical_not(is_me(to_dp, to_seq + h)))
            def _():
                inward(t, h, slot).start()

    @pl.loop(1, SEQ)
    def _(k):
        second(lax.rem(me + k, SEQ), me).wait_send()

    def swap(t):
        return pltpu.make_async_remote_copy(
            src_ref=mine.at[t + 1], dst_ref=theirs.at[t], send_sem=s_swap.at[t], recv_sem=r_swap.at[t],
            device_id=sibling, device_id_type=MESH)

    for t in (1, 0, 2):
        @pl.loop(0, HEADS)
        def _(i):
            inward(t, 0, i).wait_recv()

        if t > 0:
            swap(t - 1).start()

    def scan(queries, keys, values):
        s = jnp.dot(queries, keys, preferred_element_type=F32)
        m = jnp.max(s, axis=1, keepdims=True)
        p = jnp.exp2(s - m).astype(BF16)
        o = lax.dot_general(p, values, (((1,), (1,)), ((), ())), preferred_element_type=F32)
        return m, o

    @pl.loop(0, 2048 // QB)
    def _(b):
        q = mine[0, :, pl.ds(pl.multiple_of(b * QB, QB), QB)].astype(F32).T.astype(BF16)
        m, o = scan(q, mine[1], mine[2])
        here = pl.ds(pl.multiple_of(b * QB, QB), QB)
        peak[here, :] = jnp.broadcast_to(m, (QB, 128))
        acc[here, :] = o

    swap(0).wait_recv()
    swap(1).wait_recv()

    @pl.loop(0, 2048 // QB)
    def _(b):
        q = mine[0, :, pl.ds(pl.multiple_of(b * QB, QB), QB)].astype(F32).T.astype(BF16)
        m2, o2 = scan(q, theirs[0], theirs[1])
        here = pl.ds(pl.multiple_of(b * QB, QB), QB)
        m1 = peak[here, :][:, :1]
        o1 = acc[here, :]
        m = jnp.maximum(m1, m2)
        o = o1 * jnp.exp2(m1 - m) + o2 * jnp.exp2(m2 - m)
        o = o / o[:, HEAD : HEAD + 1]
        for j in range(QB // TOK):
            i = b * (QB // TOK) + j
            back[i] = o[j * TOK : j * TOK + TOK, :].T[:HEAD].astype(BF16)

            @pl.when(is_me(from_dp, 2 * i + core))
            def _():
                pltpu.make_async_copy(back.at[i], heads.at[head_rows(head), :], r_back.at[head]).start()

            @pl.when(jnp.logical_not(is_me(from_dp, 2 * i + core)))
            def _():
                backward(i, head).start()

    for one in loads[6:]:
        one.wait()

    @pl.loop(0, HEADS)
    def _(h):
        backward(0, h).wait_recv()

    attended = jnp.concatenate(
        [heads[j * 128 : j * 128 + 128, :].astype(F32).T.astype(BF16) for j in range(10)], axis=1)
    middle = embedded[...] + jnp.dot(attended, outw[...], preferred_element_type=F32)
    embedded[...] = middle
    normed[...] = layer_norm(middle, gain_mlp[...])

    def chunk(c):
        return pl.ds(c * ROWS, ROWS)

    def remote(src, dst, s, r, device):
        return pltpu.make_async_remote_copy(
            src_ref=src, dst_ref=dst, send_sem=s, recv_sem=r, device_id=device, device_id_type=MESH)

    def to_far(c):
        return remote(normed.at[chunk(c)], far_tok.at[chunk(c)], s_far.at[c], r_far.at[c], partner)

    def relay(c):
        return remote(far_tok.at[chunk(c)], far_near.at[chunk(c)], s_relay.at[c], r_relay.at[c], sibling)

    def swap_sum(c):
        return remote(giveswap.at[chunk(c)], fromswap.at[chunk(c)], s_gs.at[c], r_gs.at[c], sibling)

    def send_sum(c):
        return remote(giveback.at[chunk(c)], fromfar.at[chunk(c)], s_gb.at[c], r_gb.at[c], partner)

    to_near = remote(normed, near_tok, s_near, r_near, sibling)
    give_near = remote(give, fromnear, s_give, r_give, sibling)

    def mlp(x):
        hidden = gelu(jnp.dot(x, upw[...], preferred_element_type=F32)).astype(BF16)
        return jnp.dot(hidden, downw[...], preferred_element_type=F32)

    for c in range(CHUNKS):
        to_far(c).start()
    to_near.start()
    to_near.wait_recv()
    own = mlp(jnp.concatenate([normed[...], near_tok[...]], axis=0))
    total[...] = embedded[...] + own[:TOK]
    give[...] = own[TOK:].astype(BF16)
    give_near.start()

    to_far(0).wait_recv()
    relay(0).start()
    for c in range(CHUNKS):
        relay(c).wait_recv()
        sums = mlp(jnp.concatenate([far_tok[chunk(c), :], far_near[chunk(c), :]], axis=0))
        giveswap[chunk(c), :] = sums[ROWS:].astype(BF16)
        swap_sum(c).start()
        if c + 1 < CHUNKS:
            to_far(c + 1).wait_recv()
            relay(c + 1).start()
        swap_sum(c).wait_recv()
        giveback[chunk(c), :] = (sums[:ROWS] + fromswap[chunk(c), :].astype(F32)).astype(BF16)
        send_sum(c).start()

    give_near.wait_recv()
    total[...] = total[...] + fromnear[...].astype(F32)
    for c in range(CHUNKS):
        send_sum(c).wait_recv()
        result[chunk(c), :] = (total[chunk(c), :] + fromfar[chunk(c), :].astype(F32)).astype(BF16)

    to_near.wait_send()
    give_near.wait_send()
    swap(0).wait_send()
    swap(1).wait_send()
    for c in range(CHUNKS):
        to_far(c).wait_send()
        relay(c).wait_send()
        swap_sum(c).wait_send()
        send_sum(c).wait_send()

    @pl.loop(0, HEADS)
    def _(h):
        @pl.when(jnp.logical_not(is_me(to_dp, to_seq + h)))
        def _():
            for t in range(3):
                inward(t, h, 0).wait_send()

        @pl.when(jnp.logical_not(is_me(from_dp, 2 * h + core)))
        def _():
            backward(h, 0).wait_send()


def shards(images, boxes, w_embed, pos_embed, gain_attn, w_qkv, w_attn_out, gain_mlp, w_up, w_down):
    smem = pl.BlockSpec(memory_space=pltpu.SMEM)
    vmem = pl.BlockSpec(memory_space=pltpu.VMEM)
    hbm = pl.BlockSpec(memory_space=pl.ANY)
    sem = pltpu.SemaphoreType.DMA
    V = pltpu.VMEM
    out = pl.pallas_call(
        layer_kernel,
        out_shape=jax.ShapeDtypeStruct((TOK, WIDTH), BF16),
        in_specs=[smem, hbm, hbm, hbm, vmem, hbm, hbm, vmem, hbm, hbm],
        out_specs=vmem,
        scratch_shapes=[
            V((96, 1024), BF16), V((588, WIDTH), BF16), V((TOK, WIDTH), BF16), V((WIDTH, 3 * WIDTH), BF16),
            V((WIDTH, WIDTH), BF16), V((WIDTH, WIDTH), BF16), V((WIDTH, WIDTH), BF16), sem((9,)),
            V((1024, 1024), BF16), V((96, 1024), F32), V((SEQ, 32, 128), BF16), V((SEQ, 32, 128), BF16),
            V((1024, 1024), BF16), V((SEQ, 2, 16, 128), BF16), V((SEQ, 2, 16, 128), BF16),
            V((1024, 128), F32), V((TOK, OUT), BF16), V((OUT, WIDTH), BF16), V((TOK, WIDTH), F32),
            sem((SEQ,)), sem((SEQ,)), sem((SEQ,)), sem((SEQ,)),
            V((3, WIDTH, TOK), BF16), V((3, 96, 2048), BF16), V((2, 96, 2048), BF16), V((2048, 96), F32),
            V((2048, 128), F32), V((16, HEAD, TOK), BF16), V((WIDTH, TOK), BF16),
            sem((3, 16)), sem((3, 16)), sem((2,)), sem((2,)), sem((16,)), sem((16,)),
            V((TOK, WIDTH), BF16), V((TOK, WIDTH), BF16), V((TOK, WIDTH), BF16), V((TOK, WIDTH), BF16),
            V((TOK, WIDTH), F32), V((TOK, WIDTH), BF16), V((TOK, WIDTH), BF16), V((TOK, WIDTH), BF16),
            V((TOK, WIDTH), BF16), V((TOK, WIDTH), BF16), V((TOK, WIDTH), BF16),
            sem, sem, sem((CHUNKS,)), sem((CHUNKS,)), sem((CHUNKS,)), sem((CHUNKS,)), sem, sem,
            sem((CHUNKS,)), sem((CHUNKS,)), sem((CHUNKS,)), sem((CHUNKS,)),
        ],
        compiler_params=pltpu.CompilerParams(
            collective_id=0, has_side_effects=True, vmem_limit_bytes=60 * 1024 * 1024),
        name="layer",
    )(boxes, images, w_embed, pos_embed, gain_attn[None], w_qkv, w_attn_out, gain_mlp[None], w_up, w_down)
    return out[None]


def solution(mesh):
    return jax.shard_map(
        shards,
        mesh=mesh,
        in_specs=(
            P("dp", None, "seq", None), P(), P(), P("seq", None), P(), P(), P(), P(),
            P(None, "dp"), P("dp", None),
        ),
        out_specs=P("dp", "seq", None),
        check_vma=False,
    )
```

time: 172 us -> 92.1 us (0.54)
  the two profiles are of different devices: /device:TPU:0 before, /device:TPU:39 now
where the time goes in v2:
time: 92.1 us; the launch traced here: 91.8 us
  Pallas kernels  87.5 us (95%)
  local copies, waits for them, and re-layouts  4.3 us (5%)
    pallas_call x1, Pallas kernels, shards(): pl.pallas_call(layer_kernel, out_shape=jax.ShapeDtypeStruct((TOK, WIDTH),...  87.5 us

profile of v2, /device:TPU:39, one launch (start us, length us, event | category | flops | bytes accessed | tf_op | source)
XLA Modules:
  0.0 91.8 jit_solution(16086196958543592863)
XLA Ops:
  0.0 1.3 %broadcast_in_dim.9.gain_attn = f32[1,1280]{1,0:T(1,128)} reshape(f32[1280]{0:T(1024)} %param.14) | data formatting | bytes 10240 | tf_op jit(solution)/shard_map/broadcast_in_dim | solution.py:430
  1.3 1.3 %broadcast_in_dim.10.gain_mlp = f32[1,1280]{1,0:T(1,128)} reshape(f32[1280]{0:T(1024)} %param.17) | data formatting | bytes 10240 | tf_op jit(solution)/shard_map/broadcast_in_dim | solution.py:430
  2.6 87.5 %layer.1 = bf16[128,1280]{1,0:T(8,128)(2,1)} custom-call(s32[4,4]{1,0:T(4,128)} %boxes.1, bf16[1,3,32,1024]{3,2,1,0:T(8,128)(2,1)} %images.1, bf16[588,1280]{1,0:T(8,128)(2,1)} %w_embed.1, bf16[128,1280]{1,0:T(8,128)(2,1)} %pos_embed.1, f32[1,1280]{1,0:T(1,128)} %broadcast_in_dim.9.gain_attn, bf16[1280,3840]{1,0:T(8,128)(2,1)} %w_qkv.1, ...), custom_call_target="tpu_custom_call" | custom-call | tf_op jit(solution)/shard_map/layer/pallas_call | solution.py:406
  90.1 1.7 %copy.12 = bf16[1,128,1280]{2,1,0:T(8,128)(2,1)} copy(bf16[1,128,1280]{2,1,0:T(8,128)(2,1)} %bitcast.1) | data formatting | bytes 655360

commit v3 on v2

--- a/solution.py
+++ b/solution.py
@@ -43,7 +43,8 @@
     return 0.5 * x * (1.0 + lax.erf(x * (1.0 / math.sqrt(2.0))))
 
 
-QB = 256
+QB = 1024
+KB = 512
 CHUNKS = 2
 ROWS = TOK // CHUNKS
 
@@ -53,8 +54,7 @@
     img, emb, pos, qkv, outw, upw, downw, load,
     wcol, cmat, send1, recv1, wrow, send2, recv2, wide, tokens, embw, embedded, s1, r1, s2, r2,
     flat, mine, theirs, acc, peak, back, heads, s_in, r_in, s_swap, r_swap, s_back, r_back,
-    normed, near_tok, far_tok, far_near, total, give, fromnear, giveswap, fromswap, giveback, fromfar,
-    s_near, r_near, s_far, r_far, s_relay, r_relay, s_give, r_give, s_gs, r_gs, s_gb, r_gb,
+    normed, far_tok, total, giveback, fromfar, upw2, downw2, s_far, r_far, s_gb, r_gb, s_w, r_w,
 ):
     dp, me = lax.axis_index("dp"), lax.axis_index("seq")
     core, base = lax.rem(dp, 2), dp - lax.rem(dp, 2)
@@ -75,7 +75,7 @@
             (images.at[0, 2], img.at[pl.ds(64, 32)]), (w_embed, emb), (pos_embed, pos), (w_qkv, qkv),
             (w_out, outw), (w_up, upw), (w_down, downw)))
     ]
-    for one in loads:
+    for one in loads[:5]:
         one.start()
 
     barrier = pltpu.get_barrier_semaphore()
@@ -99,6 +99,12 @@
 
     greet(*sibling)
     greet(*partner)
+
+    def remote(src, dst, s, r, device):
+        return pltpu.make_async_remote_copy(
+            src_ref=src, dst_ref=dst, send_sem=s, recv_sem=r, device_id=device, device_id_type=MESH)
+
+    other = [remote(w_up, upw2, s_w.at[0], r_w.at[0], sibling), remote(w_down, downw2, s_w.at[1], r_w.at[1], sibling)]
 
     top, left, height, width = boxes[dp, 0], boxes[dp, 1], boxes[dp, 2], boxes[dp, 3]
 
@@ -148,6 +154,7 @@
     def _(k):
         first(lax.rem(me + k, SEQ), me).start()
 
+    loads[5].start()
     recv1[me] = send1[me]
 
     @pl.loop(0, 8)
@@ -208,7 +215,7 @@
             tokens[a2 * 64 : a2 * 64 + 64, kt * 128 : kt * 128 + 128] = piece.astype(BF16)
 
     embedded[...] = jnp.dot(tokens[...], embw[...], preferred_element_type=F32) + pos[...].astype(F32)
-    normed[...] = layer_norm(embedded[...], gain_attn[...])
+    normed[...] = layer_norm(embedded[...], gain_attn[...].reshape(1, WIDTH))
 
     def head_rows(h):
         return pl.ds(pl.multiple_of(h * HEAD, 16), HEAD)
@@ -228,76 +235,127 @@
             send_sem=s_back.at[i], recv_sem=r_back.at[h],
             device_id=(from_dp, 2 * i + core), device_id_type=MESH)
 
-    loads[5].wait()
-    for t in (1, 0, 2):
+    def turn(k):
+        return lax.rem(slot // 4 + k // 4, 4) * 4 + lax.rem(slot + k, 4)
+
+    def post(ts, first_k, last_k):
+        @pl.loop(first_k, last_k)
+        def _(k):
+            h = turn(k)
+
+            @pl.when(is_me(to_dp, to_seq + h))
+            def _():
+                for t in ts:
+                    pltpu.make_async_copy(
+                        flat.at[t, head_rows(h), :], mine.at[t, pl.ds(0, HEAD), lanes(slot)],
+                        r_in.at[t, slot]).start()
+
+            @pl.when(jnp.logical_not(is_me(to_dp, to_seq + h)))
+            def _():
+                for t in ts:
+                    inward(t, h, slot).start()
+
+    def posted(ts, first_k, last_k):
+        @pl.loop(first_k, last_k)
+        def _(k):
+            h = turn(k)
+
+            @pl.when(jnp.logical_not(is_me(to_dp, to_seq + h)))
+            def _():
+                for t in ts:
+                    inward(t, h, slot).wait_send()
+
+    def project(t, scale):
         proj = jnp.dot(normed[...], qkv[:, t * WIDTH : (t + 1) * WIDTH], preferred_element_type=F32)
-        if t == 0:
-            proj = proj * (math.log2(math.e) / math.sqrt(HEAD))
+        if scale is not None:
+            proj = proj * scale
         for j in range(10):
             flat[t, j * 128 : j * 128 + 128, :] = proj[:, j * 128 : j * 128 + 128].T.astype(BF16)
 
-        @pl.loop(0, HEADS)
-        def _(k):
-            h = lax.rem(slot + k, HEADS)
-
-            @pl.when(is_me(to_dp, to_seq + h))
-            def _():
-                pltpu.make_async_copy(
-                    flat.at[t, head_rows(h), :], mine.at[t, pl.ds(0, HEAD), lanes(slot)],
-                    r_in.at[t, slot]).start()
-
-            @pl.when(jnp.logical_not(is_me(to_dp, to_seq + h)))
-            def _():
-                inward(t, h, slot).start()
+    loads[5].wait()
+    project(0, math.log2(math.e) / math.sqrt(HEAD))
+    post((0,), 0, 16)
+    project(1, None)
+    project(2, None)
+    post((1, 2), 0, 4)
 
     @pl.loop(1, SEQ)
     def _(k):
         second(lax.rem(me + k, SEQ), me).wait_send()
 
-    def swap(t):
-        return pltpu.make_async_remote_copy(
-            src_ref=mine.at[t + 1], dst_ref=theirs.at[t], send_sem=s_swap.at[t], recv_sem=r_swap.at[t],
-            device_id=sibling, device_id_type=MESH)
-
-    for t in (1, 0, 2):
-        @pl.loop(0, HEADS)
-        def _(i):
-            inward(t, 0, i).wait_recv()
-
-        if t > 0:
-            swap(t - 1).start()
-
-    def scan(queries, keys, values):
-        s = jnp.dot(queries, keys, preferred_element_type=F32)
-        m = jnp.max(s, axis=1, keepdims=True)
-        p = jnp.exp2(s - m).astype(BF16)
-        o = lax.dot_general(p, values, (((1,), (1,)), ((), ())), preferred_element_type=F32)
-        return m, o
-
-    @pl.loop(0, 2048 // QB)
-    def _(b):
-        q = mine[0, :, pl.ds(pl.multiple_of(b * QB, QB), QB)].astype(F32).T.astype(BF16)
-        m, o = scan(q, mine[1], mine[2])
-        here = pl.ds(pl.multiple_of(b * QB, QB), QB)
-        peak[here, :] = jnp.broadcast_to(m, (QB, 128))
-        acc[here, :] = o
-
-    swap(0).wait_recv()
-    swap(1).wait_recv()
-
-    @pl.loop(0, 2048 // QB)
-    def _(b):
-        q = mine[0, :, pl.ds(pl.multiple_of(b * QB, QB), QB)].astype(F32).T.astype(BF16)
-        m2, o2 = scan(q, theirs[0], theirs[1])
-        here = pl.ds(pl.multiple_of(b * QB, QB), QB)
-        m1 = peak[here, :][:, :1]
-        o1 = acc[here, :]
-        m = jnp.maximum(m1, m2)
-        o = o1 * jnp.exp2(m1 - m) + o2 * jnp.exp2(m2 - m)
-        o = o / o[:, HEAD : HEAD + 1]
+    for one in loads[6:]:
+        one.start()
+    for one in other:
+        one.start()
+    posted((0,), 0, 16)
+    post((1, 2), 4, 8)
+
+    def keys_of(g):
+        return pl.ds(pl.multiple_of(g * KB, KB), KB)
+
+    def swap(g):
+        return pltpu.make_async_remote_copy(
+            src_ref=mine.at[pl.ds(1, 2), :, keys_of(g)], dst_ref=theirs.at[:, :, keys_of(g)],
+            send_sem=s_swap.at[g], recv_sem=r_swap.at[g], device_id=sibling, device_id_type=MESH)
+
+    @pl.loop(0, HEADS)
+    def _(i):
+        inward(0, 0, i).wait_recv()
+
+    peak[...] = jnp.full((8, 2048), -jnp.inf, F32)
+    acc[...] = jnp.zeros((96, 2048), F32)
+
+    def group(step):
+        return lax.rem(head // 4 + 4 - step, 4)
+
+    def take(keys, values, here):
+        rows = keys.astype(F32).T.astype(BF16)
+        s = jnp.dot(rows, mine[0, :, here], preferred_element_type=F32)
+        old = peak[:1, here]
+        new = jnp.maximum(old, jnp.max(s, axis=0, keepdims=True))
+        p = jnp.exp2(s - new).astype(BF16)
+        return new, acc[:, here] * jnp.exp2(old - new) + jnp.dot(values, p, preferred_element_type=F32)
+
+    def absorb(keys, values):
+        new, sums = take(keys, values, slice(0, 2048))
+        acc[...] = sums
+        peak[...] = jnp.broadcast_to(new, (8, 2048))
+
+    @pl.loop(0, 4)
+    def _(step):
+        g = group(step)
+
+        @pl.when(step < 2)
+        def _():
+            posted((1, 2), step * 4, step * 4 + 4)
+            post((1, 2), step * 4 + 8, step * 4 + 12)
+
+        for j in range(4):
+            for t in (1, 2):
+                inward(t, 0, g * 4 + j).wait_recv()
+        swap(g).start()
+        absorb(mine[1, :, keys_of(g)], mine[2, :, keys_of(g)])
+
+        @pl.when(step > 0)
+        def _():
+            earlier = group(step - 1)
+            swap(earlier).wait_recv()
+            absorb(theirs[0, :, keys_of(earlier)], theirs[1, :, keys_of(earlier)])
+
+    last = group(3)
+    swap(last).wait_recv()
+    for step in range(2048 // QB):
+        b = lax.rem(step + head, 2048 // QB)
+        _, o = take(
+            theirs[0, :, keys_of(last)], theirs[1, :, keys_of(last)],
+            pl.ds(pl.multiple_of(b * QB, QB), QB))
+        o = (o[:HEAD] / o[HEAD : HEAD + 1]).astype(BF16)
         for j in range(QB // TOK):
-            i = b * (QB // TOK) + j
-            back[i] = o[j * TOK : j * TOK + TOK, :].T[:HEAD].astype(BF16)
+            back[b * (QB // TOK) + j] = o[:, j * TOK : j * TOK + TOK]
+
+        @pl.loop(0, QB // TOK)
+        def _(j):
+            i = b * (QB // TOK) + lax.rem(j + head, QB // TOK)
 
             @pl.when(is_me(from_dp, 2 * i + core))
             def _():
@@ -318,80 +376,49 @@
         [heads[j * 128 : j * 128 + 128, :].astype(F32).T.astype(BF16) for j in range(10)], axis=1)
     middle = embedded[...] + jnp.dot(attended, outw[...], preferred_element_type=F32)
     embedded[...] = middle
-    normed[...] = layer_norm(middle, gain_mlp[...])
+    normed[...] = layer_norm(middle, gain_mlp[...].reshape(1, WIDTH))
 
     def chunk(c):
         return pl.ds(c * ROWS, ROWS)
 
-    def remote(src, dst, s, r, device):
-        return pltpu.make_async_remote_copy(
-            src_ref=src, dst_ref=dst, send_sem=s, recv_sem=r, device_id=device, device_id_type=MESH)
-
     def to_far(c):
         return remote(normed.at[chunk(c)], far_tok.at[chunk(c)], s_far.at[c], r_far.at[c], partner)
 
-    def relay(c):
-        return remote(far_tok.at[chunk(c)], far_near.at[chunk(c)], s_relay.at[c], r_relay.at[c], sibling)
-
-    def swap_sum(c):
-        return remote(giveswap.at[chunk(c)], fromswap.at[chunk(c)], s_gs.at[c], r_gs.at[c], sibling)
-
     def send_sum(c):
         return remote(giveback.at[chunk(c)], fromfar.at[chunk(c)], s_gb.at[c], r_gb.at[c], partner)
 
-    to_near = remote(normed, near_tok, s_near, r_near, sibling)
-    give_near = remote(give, fromnear, s_give, r_give, sibling)
-
     def mlp(x):
-        hidden = gelu(jnp.dot(x, upw[...], preferred_element_type=F32)).astype(BF16)
-        return jnp.dot(hidden, downw[...], preferred_element_type=F32)
+        sums = None
+        for up, down in ((upw, downw), (upw2, downw2)):
+            hidden = gelu(jnp.dot(x, up[...], preferred_element_type=F32)).astype(BF16)
+            part = jnp.dot(hidden, down[...], preferred_element_type=F32)
+            sums = part if sums is None else sums + part
+        return sums
 
     for c in range(CHUNKS):
         to_far(c).start()
-    to_near.start()
-    to_near.wait_recv()
-    own = mlp(jnp.concatenate([normed[...], near_tok[...]], axis=0))
-    total[...] = embedded[...] + own[:TOK]
-    give[...] = own[TOK:].astype(BF16)
-    give_near.start()
-
-    to_far(0).wait_recv()
-    relay(0).start()
+    for one in other:
+        one.wait_recv()
+    total[...] = embedded[...] + mlp(normed[...])
     for c in range(CHUNKS):
-        relay(c).wait_recv()
-        sums = mlp(jnp.concatenate([far_tok[chunk(c), :], far_near[chunk(c), :]], axis=0))
-        giveswap[chunk(c), :] = sums[ROWS:].astype(BF16)
-        swap_sum(c).start()
-        if c + 1 < CHUNKS:
-            to_far(c + 1).wait_recv()
-            relay(c + 1).start()
-        swap_sum(c).wait_recv()
-        giveback[chunk(c), :] = (sums[:ROWS] + fromswap[chunk(c), :].astype(F32)).astype(BF16)
+        to_far(c).wait_recv()
+        giveback[chunk(c), :] = mlp(far_tok[chunk(c), :]).astype(BF16)
         send_sum(c).start()
-
-    give_near.wait_recv()
-    total[...] = total[...] + fromnear[...].astype(F32)
     for c in range(CHUNKS):
         send_sum(c).wait_recv()
         result[chunk(c), :] = (total[chunk(c), :] + fromfar[chunk(c), :].astype(F32)).astype(BF16)
 
-    to_near.wait_send()
-    give_near.wait_send()
-    swap(0).wait_send()
-    swap(1).wait_send()
+    posted((1, 2), 8, 16)
+    for one in other:
+        one.wait_send()
+    for g in range(4):
+        swap(g).wait_send()
     for c in range(CHUNKS):
         to_far(c).wait_send()
-        relay(c).wait_send()
-        swap_sum(c).wait_send()
         send_sum(c).wait_send()
 
     @pl.loop(0, HEADS)
     def _(h):
-        @pl.when(jnp.logical_not(is_me(to_dp, to_seq + h)))
-        def _():
-            for t in range(3):
-                inward(t, h, 0).wait_send()
-
         @pl.when(jnp.logical_not(is_me(from_dp, 2 * h + core)))
         def _():
             backward(h, 0).wait_send()
@@ -415,19 +442,17 @@
             V((1024, 1024), BF16), V((SEQ, 2, 16, 128), BF16), V((SEQ, 2, 16, 128), BF16),
             V((1024, 128), F32), V((TOK, OUT), BF16), V((OUT, WIDTH), BF16), V((TOK, WIDTH), F32),
             sem((SEQ,)), sem((SEQ,)), sem((SEQ,)), sem((SEQ,)),
-            V((3, WIDTH, TOK), BF16), V((3, 96, 2048), BF16), V((2, 96, 2048), BF16), V((2048, 96), F32),
-            V((2048, 128), F32), V((16, HEAD, TOK), BF16), V((WIDTH, TOK), BF16),
-            sem((3, 16)), sem((3, 16)), sem((2,)), sem((2,)), sem((16,)), sem((16,)),
-            V((TOK, WIDTH), BF16), V((TOK, WIDTH), BF16), V((TOK, WIDTH), BF16), V((TOK, WIDTH), BF16),
-            V((TOK, WIDTH), F32), V((TOK, WIDTH), BF16), V((TOK, WIDTH), BF16), V((TOK, WIDTH), BF16),
-            V((TOK, WIDTH), BF16), V((TOK, WIDTH), BF16), V((TOK, WIDTH), BF16),
-            sem, sem, sem((CHUNKS,)), sem((CHUNKS,)), sem((CHUNKS,)), sem((CHUNKS,)), sem, sem,
-            sem((CHUNKS,)), sem((CHUNKS,)), sem((CHUNKS,)), sem((CHUNKS,)),
+            V((3, WIDTH, TOK), BF16), V((3, 96, 2048), BF16), V((2, 96, 2048), BF16),
+            V((96, 2048), F32), V((8, 2048), F32), V((16, HEAD, TOK), BF16), V((WIDTH, TOK), BF16),
+            sem((3, 16)), sem((3, 16)), sem((4,)), sem((4,)), sem((16,)), sem((16,)),
+            V((TOK, WIDTH), BF16), V((TOK, WIDTH), BF16), V((TOK, WIDTH), F32), V((TOK, WIDTH), BF16),
+            V((TOK, WIDTH), BF16), V((WIDTH, WIDTH), BF16), V((WIDTH, WIDTH), BF16),
+            sem((CHUNKS,)), sem((CHUNKS,)), sem((CHUNKS,)), sem((CHUNKS,)), sem((2,)), sem((2,)),
         ],
         compiler_params=pltpu.CompilerParams(
             collective_id=0, has_side_effects=True, vmem_limit_bytes=60 * 1024 * 1024),
         name="layer",
-    )(boxes, images, w_embed, pos_embed, gain_attn[None], w_qkv, w_attn_out, gain_mlp[None], w_up, w_down)
+    )(boxes, images, w_embed, pos_embed, gain_attn, w_qkv, w_attn_out, gain_mlp, w_up, w_down)
     return out[None]
 
 

time: 92.1 us -> 80.3 us (0.87)
  the two profiles are of different devices: /device:TPU:39 before, /device:TPU:0 now
where the time goes in v3:
time: 80.3 us; the launch traced here: 80.2 us
  Pallas kernels  78.4 us (98%)
  local copies, waits for them, and re-layouts  1.72 us (2%)
    pallas_call x1, Pallas kernels, shards(): pl.pallas_call(layer_kernel, out_shape=jax.ShapeDtypeStruct((TOK, WIDTH),...  78.4 us
    unnamed x1, local copies, waits for them, and re-layouts  1.72 us

profile of v3, /device:TPU:0, one launch (start us, length us, event | category | flops | bytes accessed | tf_op | source)
XLA Modules:
  0.0 80.2 jit_solution(18030840045814434464)
XLA Ops:
  0.0 78.4 %layer.1 = bf16[128,1280]{1,0:T(8,128)(2,1)} custom-call(s32[4,4]{1,0:T(4,128)} %boxes.1, bf16[1,3,32,1024]{3,2,1,0:T(8,128)(2,1)} %images.1, bf16[588,1280]{1,0:T(8,128)(2,1)} %w_embed.1, bf16[128,1280]{1,0:T(8,128)(2,1)} %pos_embed.1, f32[1280]{0:T(1024)} %gain_attn.1, bf16[1280,3840]{1,0:T(8,128)(2,1)} %w_qkv.1, bf16[1280,1280]{1,0:T(8,128)(2,1)} %w_out.1, ...), custom_call_target="tpu_custom_call" | custom-call | tf_op jit(solution)/shard_map/layer/pallas_call | solution.py:433
  78.5 1.7 %copy.12 = bf16[1,128,1280]{2,1,0:T(8,128)(2,1)} copy(bf16[1,128,1280]{2,1,0:T(8,128)(2,1)} %bitcast.1) | data formatting | bytes 655360

commit v4 on v3

--- a/solution.py
+++ b/solution.py
@@ -50,8 +50,8 @@
 
 
 def layer_kernel(
-    boxes, images, w_embed, pos_embed, gain_attn, w_qkv, w_out, gain_mlp, w_up, w_down, result,
-    img, emb, pos, qkv, outw, upw, downw, load,
+    boxes_in, images, w_embed, pos_embed, gain_in, w_qkv, w_out, gain2_in, w_up, w_down, result,
+    boxes, gain_attn, gain_mlp, small, img, emb, pos, qkv, outw, upw, downw, load,
     wcol, cmat, send1, recv1, wrow, send2, recv2, wide, tokens, embw, embedded, s1, r1, s2, r2,
     flat, mine, theirs, acc, peak, back, heads, s_in, r_in, s_swap, r_swap, s_back, r_back,
     normed, far_tok, total, giveback, fromfar, upw2, downw2, s_far, r_far, s_gb, r_gb, s_w, r_w,
@@ -68,6 +68,35 @@
     def is_me(d, s):
         return jnp.logical_and(d == dp, s == me)
 
+    barrier = pltpu.get_barrier_semaphore()
+
+    def greet(d, s):
+        pl.semaphore_signal(barrier, inc=1, device_id=(d, s), device_id_type=MESH)
+
+    @pl.loop(1, SEQ)
+    def _(k):
+        greet(dp, lax.rem(me + k, SEQ))
+
+    @pl.loop(0, HEADS)
+    def _(h):
+        @pl.when(jnp.logical_not(is_me(to_dp, to_seq + h)))
+        def _():
+            greet(to_dp, to_seq + h)
+
+        @pl.when(jnp.logical_not(is_me(from_dp, 2 * h + core)))
+        def _():
+            greet(from_dp, 2 * h + core)
+
+    greet(*sibling)
+    greet(*partner)
+
+    smalls = [
+        pltpu.make_async_copy(a, b, small.at[i])
+        for i, (a, b) in enumerate(((boxes_in, boxes), (gain_in, gain_attn), (gain2_in, gain_mlp)))
+    ]
+    for one in smalls:
+        one.start()
+
     loads = [
         pltpu.make_async_copy(a, b, load.at[i])
         for i, (a, b) in enumerate((
@@ -78,34 +107,14 @@
     for one in loads[:5]:
         one.start()
 
-    barrier = pltpu.get_barrier_semaphore()
-
-    def greet(d, s):
-        pl.semaphore_signal(barrier, inc=1, device_id=(d, s), device_id_type=MESH)
-
-    @pl.loop(1, SEQ)
-    def _(k):
-        greet(dp, lax.rem(me + k, SEQ))
-
-    @pl.loop(0, HEADS)
-    def _(h):
-        @pl.when(jnp.logical_not(is_me(to_dp, to_seq + h)))
-        def _():
-            greet(to_dp, to_seq + h)
-
-        @pl.when(jnp.logical_not(is_me(from_dp, 2 * h + core)))
-        def _():
-            greet(from_dp, 2 * h + core)
-
-    greet(*sibling)
-    greet(*partner)
-
     def remote(src, dst, s, r, device):
         return pltpu.make_async_remote_copy(
             src_ref=src, dst_ref=dst, send_sem=s, recv_sem=r, device_id=device, device_id_type=MESH)
 
     other = [remote(w_up, upw2, s_w.at[0], r_w.at[0], sibling), remote(w_down, downw2, s_w.at[1], r_w.at[1], sibling)]
 
+    for one in smalls:
+        one.wait()
     top, left, height, width = boxes[dp, 0], boxes[dp, 1], boxes[dp, 2], boxes[dp, 3]
 
     @pl.loop(0, 8)
@@ -223,9 +232,12 @@
     def lanes(i):
         return pl.ds(pl.multiple_of(i * TOK, TOK), TOK)
 
+    def span(t):
+        return pl.ds(t, 1 + t)
+
     def inward(t, h, i):
         return pltpu.make_async_remote_copy(
-            src_ref=flat.at[t, head_rows(h), :], dst_ref=mine.at[t, pl.ds(0, HEAD), lanes(i)],
+            src_ref=flat.at[span(t), head_rows(h), :], dst_ref=mine.at[span(t), pl.ds(0, HEAD), lanes(i)],
             send_sem=s_in.at[t, h], recv_sem=r_in.at[t, i],
             device_id=(to_dp, to_seq + h), device_id_type=MESH)
 
@@ -247,7 +259,7 @@
             def _():
                 for t in ts:
                     pltpu.make_async_copy(
-                        flat.at[t, head_rows(h), :], mine.at[t, pl.ds(0, HEAD), lanes(slot)],
+                        flat.at[span(t), head_rows(h), :], mine.at[span(t), pl.ds(0, HEAD), lanes(slot)],
                         r_in.at[t, slot]).start()
 
             @pl.when(jnp.logical_not(is_me(to_dp, to_seq + h)))
@@ -277,7 +289,7 @@
     post((0,), 0, 16)
     project(1, None)
     project(2, None)
-    post((1, 2), 0, 4)
+    post((1,), 0, 4)
 
     @pl.loop(1, SEQ)
     def _(k):
@@ -288,7 +300,7 @@
     for one in other:
         one.start()
     posted((0,), 0, 16)
-    post((1, 2), 4, 8)
+    post((1,), 4, 8)
 
     def keys_of(g):
         return pl.ds(pl.multiple_of(g * KB, KB), KB)
@@ -308,47 +320,51 @@
     def group(step):
         return lax.rem(head // 4 + 4 - step, 4)
 
-    def take(keys, values, here):
+    def take(keys, values, q, old, sums):
         rows = keys.astype(F32).T.astype(BF16)
-        s = jnp.dot(rows, mine[0, :, here], preferred_element_type=F32)
-        old = peak[:1, here]
+        s = jnp.dot(rows, q, preferred_element_type=F32)
         new = jnp.maximum(old, jnp.max(s, axis=0, keepdims=True))
         p = jnp.exp2(s - new).astype(BF16)
-        return new, acc[:, here] * jnp.exp2(old - new) + jnp.dot(values, p, preferred_element_type=F32)
-
-    def absorb(keys, values):
-        new, sums = take(keys, values, slice(0, 2048))
+        return new, sums * jnp.exp2(old - new) + jnp.dot(values, p, preferred_element_type=F32)
+
+    def arrived(g):
+        for j in range(4):
+            inward(1, 0, g * 4 + j).wait_recv()
+        swap(g).start()
+
+    def keep(new, sums):
         acc[...] = sums
         peak[...] = jnp.broadcast_to(new, (8, 2048))
 
-    @pl.loop(0, 4)
+    posted((1,), 0, 4)
+    post((1,), 8, 12)
+    begin = group(0)
+    arrived(begin)
+    keep(*take(mine[1, :, keys_of(begin)], mine[2, :, keys_of(begin)], mine[0], peak[:1, :], acc[...]))
+
+    @pl.loop(1, 4)
     def _(step):
-        g = group(step)
-
-        @pl.when(step < 2)
+        @pl.when(step == 1)
         def _():
-            posted((1, 2), step * 4, step * 4 + 4)
-            post((1, 2), step * 4 + 8, step * 4 + 12)
-
-        for j in range(4):
-            for t in (1, 2):
-                inward(t, 0, g * 4 + j).wait_recv()
-        swap(g).start()
-        absorb(mine[1, :, keys_of(g)], mine[2, :, keys_of(g)])
-
-        @pl.when(step > 0)
-        def _():
-            earlier = group(step - 1)
-            swap(earlier).wait_recv()
-            absorb(theirs[0, :, keys_of(earlier)], theirs[1, :, keys_of(earlier)])
+            posted((1,), 4, 8)
+            post((1,), 12, 16)
+
+        g, earlier = group(step), group(step - 1)
+        arrived(g)
+        swap(earlier).wait_recv()
+        keep(*take(
+            jnp.concatenate([theirs[0, :, keys_of(earlier)], mine[1, :, keys_of(g)]], axis=1),
+            jnp.concatenate([theirs[1, :, keys_of(earlier)], mine[2, :, keys_of(g)]], axis=1),
+            mine[0], peak[:1, :], acc[...]))
 
     last = group(3)
     swap(last).wait_recv()
     for step in range(2048 // QB):
         b = lax.rem(step + head, 2048 // QB)
+        here = pl.ds(pl.multiple_of(b * QB, QB), QB)
         _, o = take(
-            theirs[0, :, keys_of(last)], theirs[1, :, keys_of(last)],
-            pl.ds(pl.multiple_of(b * QB, QB), QB))
+            theirs[0, :, keys_of(last)], theirs[1, :, keys_of(last)], mine[0, :, here], peak[:1, here],
+            acc[:, here])
         o = (o[:HEAD] / o[HEAD : HEAD + 1]).astype(BF16)
         for j in range(QB // TOK):
             back[b * (QB // TOK) + j] = o[:, j * TOK : j * TOK + TOK]
@@ -384,38 +400,44 @@
     def to_far(c):
         return remote(normed.at[chunk(c)], far_tok.at[chunk(c)], s_far.at[c], r_far.at[c], partner)
 
-    def send_sum(c):
-        return remote(giveback.at[chunk(c)], fromfar.at[chunk(c)], s_gb.at[c], r_gb.at[c], partner)
-
-    def mlp(x):
-        sums = None
-        for up, down in ((upw, downw), (upw2, downw2)):
-            hidden = gelu(jnp.dot(x, up[...], preferred_element_type=F32)).astype(BF16)
-            part = jnp.dot(hidden, down[...], preferred_element_type=F32)
-            sums = part if sums is None else sums + part
-        return sums
+    parts = (pl.ds(0, 768), pl.ds(768, 512))
+
+    def send_sum(c, k):
+        return remote(
+            giveback.at[chunk(c), parts[k]], fromfar.at[chunk(c), parts[k]], s_gb.at[c, k], r_gb.at[c, k], partner)
+
+    def hidden_of(x):
+        return [gelu(jnp.dot(x, up[...], preferred_element_type=F32)).astype(BF16) for up in (upw, upw2)]
+
+    def summed(hidden, part):
+        return jnp.dot(hidden[0], downw[:, part], preferred_element_type=F32) + jnp.dot(
+            hidden[1], downw2[:, part], preferred_element_type=F32)
 
     for c in range(CHUNKS):
         to_far(c).start()
     for one in other:
         one.wait_recv()
-    total[...] = embedded[...] + mlp(normed[...])
+    total[...] = embedded[...] + summed(hidden_of(normed[...]), slice(None))
     for c in range(CHUNKS):
         to_far(c).wait_recv()
-        giveback[chunk(c), :] = mlp(far_tok[chunk(c), :]).astype(BF16)
-        send_sum(c).start()
+        hidden = hidden_of(far_tok[chunk(c), :])
+        for k, part in enumerate(parts):
+            giveback[chunk(c), part] = summed(hidden, part).astype(BF16)
+            send_sum(c, k).start()
     for c in range(CHUNKS):
-        send_sum(c).wait_recv()
+        for k in range(2):
+            send_sum(c, k).wait_recv()
         result[chunk(c), :] = (total[chunk(c), :] + fromfar[chunk(c), :].astype(F32)).astype(BF16)
 
-    posted((1, 2), 8, 16)
+    posted((1,), 8, 16)
     for one in other:
         one.wait_send()
     for g in range(4):
         swap(g).wait_send()
     for c in range(CHUNKS):
         to_far(c).wait_send()
-        send_sum(c).wait_send()
+        for k in range(2):
+            send_sum(c, k).wait_send()
 
     @pl.loop(0, HEADS)
     def _(h):
@@ -425,7 +447,6 @@
 
 
 def shards(images, boxes, w_embed, pos_embed, gain_attn, w_qkv, w_attn_out, gain_mlp, w_up, w_down):
-    smem = pl.BlockSpec(memory_space=pltpu.SMEM)
     vmem = pl.BlockSpec(memory_space=pltpu.VMEM)
     hbm = pl.BlockSpec(memory_space=pl.ANY)
     sem = pltpu.SemaphoreType.DMA
@@ -433,9 +454,10 @@
     out = pl.pallas_call(
         layer_kernel,
         out_shape=jax.ShapeDtypeStruct((TOK, WIDTH), BF16),
-        in_specs=[smem, hbm, hbm, hbm, vmem, hbm, hbm, vmem, hbm, hbm],
+        in_specs=[hbm] * 10,
         out_specs=vmem,
         scratch_shapes=[
+            pltpu.SMEM((4, 4), jnp.int32), V((WIDTH,), F32), V((WIDTH,), F32), sem((3,)),
             V((96, 1024), BF16), V((588, WIDTH), BF16), V((TOK, WIDTH), BF16), V((WIDTH, 3 * WIDTH), BF16),
             V((WIDTH, WIDTH), BF16), V((WIDTH, WIDTH), BF16), V((WIDTH, WIDTH), BF16), sem((9,)),
             V((1024, 1024), BF16), V((96, 1024), F32), V((SEQ, 32, 128), BF16), V((SEQ, 32, 128), BF16),
@@ -444,10 +466,10 @@
             sem((SEQ,)), sem((SEQ,)), sem((SEQ,)), sem((SEQ,)),
             V((3, WIDTH, TOK), BF16), V((3, 96, 2048), BF16), V((2, 96, 2048), BF16),
             V((96, 2048), F32), V((8, 2048), F32), V((16, HEAD, TOK), BF16), V((WIDTH, TOK), BF16),
-            sem((3, 16)), sem((3, 16)), sem((4,)), sem((4,)), sem((16,)), sem((16,)),
+            sem((2, 16)), sem((2, 16)), sem((4,)), sem((4,)), sem((16,)), sem((16,)),
             V((TOK, WIDTH), BF16), V((TOK, WIDTH), BF16), V((TOK, WIDTH), F32), V((TOK, WIDTH), BF16),
             V((TOK, WIDTH), BF16), V((WIDTH, WIDTH), BF16), V((WIDTH, WIDTH), BF16),
-            sem((CHUNKS,)), sem((CHUNKS,)), sem((CHUNKS,)), sem((CHUNKS,)), sem((2,)), sem((2,)),
+            sem((CHUNKS,)), sem((CHUNKS,)), sem((CHUNKS, 2)), sem((CHUNKS, 2)), sem((2,)), sem((2,)),
         ],
         compiler_params=pltpu.CompilerParams(
             collective_id=0, has_side_effects=True, vmem_limit_bytes=60 * 1024 * 1024),

time: 80.3 us -> 78.6 us (0.979)
  Pallas kernels: 78.4 us -> 76.6 us
    pallas_call x1, Pallas kernels: 78.4 us -> 76.6 us  [shards(): pl.pallas_call(layer_kernel, out_shape=jax.ShapeDtypeStruct((TOK, WIDTH),...]
where the time goes in v4:
time: 78.6 us; the launch traced here: 78.4 us
  Pallas kernels  76.6 us (97%)
  local copies, waits for them, and re-layouts  1.72 us (2%)
    pallas_call x1, Pallas kernels, shards(): pl.pallas_call(layer_kernel, out_shape=jax.ShapeDtypeStruct((TOK, WIDTH),...  76.6 us
    unnamed x1, local copies, waits for them, and re-layouts  1.72 us

profile of v4, /device:TPU:0, one launch (start us, length us, event | category | flops | bytes accessed | tf_op | source)
XLA Modules:
  0.0 78.4 jit_solution(10468034175743649640)
XLA Ops:
  0.0 76.6 %layer.1 = bf16[128,1280]{1,0:T(8,128)(2,1)} custom-call(s32[4,4]{1,0:T(4,128)} %boxes_in.1, bf16[1,3,32,1024]{3,2,1,0:T(8,128)(2,1)} %images.1, bf16[588,1280]{1,0:T(8,128)(2,1)} %w_embed.1, bf16[128,1280]{1,0:T(8,128)(2,1)} %pos_embed.1, f32[1280]{0:T(1024)} %gain_in.1, bf16[1280,3840]{1,0:T(8,128)(2,1)} %w_qkv.1, bf16[1280,1280]{1,0:T(8,128)(2,1)} %w_out.1, ...), custom_call_target="tpu_custom_call" | custom-call | tf_op jit(solution)/shard_map/layer/pallas_call | solution.py:454
  76.6 1.7 %copy.12 = bf16[1,128,1280]{2,1,0:T(8,128)(2,1)} copy(bf16[1,128,1280]{2,1,0:T(8,128)(2,1)} %bitcast.1) | data formatting | bytes 655360

commit v5 on v4

--- a/solution.py
+++ b/solution.py
@@ -183,16 +183,21 @@
         first(me, lax.rem(me + k, SEQ)).wait_recv()
 
     x = recv1[...].reshape(1024, 128)
-    even = jnp.dot(wrow[:512], x, preferred_element_type=F32)
-    odd = jnp.dot(wrow[512:], x, preferred_element_type=F32)
-    low = lax.broadcasted_iota(jnp.int32, (512, 128), 1) < 64
-    send2[:, 0] = jnp.where(low, even, pltpu.roll(odd, 64, 1)).astype(BF16).reshape(32, 16, 128)
-    send2[:, 1] = jnp.where(low, pltpu.roll(even, 64, 1), odd).astype(BF16).reshape(32, 16, 128)
-
-    @pl.loop(1, SEQ)
-    def _(k):
-        second(lax.rem(me + k, SEQ), me).start()
-
+    low = lax.broadcasted_iota(jnp.int32, (256, 128), 1) < 64
+    for i in range(2):
+        h = lax.rem(me // 16 + 1 + i, 2)
+        even = jnp.dot(wrow[pl.ds(pl.multiple_of(h * 256, 256), 256)], x, preferred_element_type=F32)
+        odd = jnp.dot(wrow[pl.ds(pl.multiple_of(h * 256 + 512, 256), 256)], x, preferred_element_type=F32)
+        to = pl.ds(h * 16, 16)
+        send2[to, 0] = jnp.where(low, even, pltpu.roll(odd, 64, 1)).astype(BF16).reshape(16, 16, 128)
+        send2[to, 1] = jnp.where(low, pltpu.roll(even, 64, 1), odd).astype(BF16).reshape(16, 16, 128)
+
+        @pl.loop(i, 16)
+        def _(k):
+            second(h * 16 + lax.rem(me + k, 16), me).start()
+
+    for one in other:
+        one.start()
     recv2[me] = send2[me]
 
     for one in loads[3:5]:
@@ -295,10 +300,6 @@
     def _(k):
         second(lax.rem(me + k, SEQ), me).wait_send()
 
-    for one in loads[6:]:
-        one.start()
-    for one in other:
-        one.start()
     posted((0,), 0, 16)
     post((1,), 4, 8)
 
@@ -357,6 +358,8 @@
             jnp.concatenate([theirs[1, :, keys_of(earlier)], mine[2, :, keys_of(g)]], axis=1),
             mine[0], peak[:1, :], acc[...]))
 
+    for one in loads[6:]:
+        one.start()
     last = group(3)
     swap(last).wait_recv()
     for step in range(2048 // QB):

time: 78.6 us -> 78 us (level)
  no operation moved by 1% of the time
where the time goes in v5:
time: 78 us; the launch traced here: 77.8 us
  Pallas kernels  76.1 us (98%)
  local copies, waits for them, and re-layouts  1.72 us (2%)
    pallas_call x1, Pallas kernels, shards(): pl.pallas_call(layer_kernel, out_shape=jax.ShapeDtypeStruct((TOK, WIDTH),...  76.1 us
    unnamed x1, local copies, waits for them, and re-layouts  1.72 us

profile of v5, /device:TPU:0, one launch (start us, length us, event | category | flops | bytes accessed | tf_op | source)
XLA Modules:
  0.0 77.8 jit_solution(1449417818529035064)
XLA Ops:
  0.0 76.1 %layer.1 = bf16[128,1280]{1,0:T(8,128)(2,1)} custom-call(s32[4,4]{1,0:T(4,128)} %boxes_in.1, bf16[1,3,32,1024]{3,2,1,0:T(8,128)(2,1)} %images.1, bf16[588,1280]{1,0:T(8,128)(2,1)} %w_embed.1, bf16[128,1280]{1,0:T(8,128)(2,1)} %pos_embed.1, f32[1280]{0:T(1024)} %gain_in.1, bf16[1280,3840]{1,0:T(8,128)(2,1)} %w_qkv.1, bf16[1280,1280]{1,0:T(8,128)(2,1)} %w_out.1, ...), custom_call_target="tpu_custom_call" | custom-call | tf_op jit(solution)/shard_map/layer/pallas_call | solution.py:457
  76.1 1.7 %copy.12 = bf16[1,128,1280]{2,1,0:T(8,128)(2,1)} copy(bf16[1,128,1280]{2,1,0:T(8,128)(2,1)} %bitcast.1) | data formatting | bytes 655360
